TPU v7x, 32 devices: a whole 2x2x4 slice. The times are simulated.
32 devices in a mesh: req: 4 (over y, x), blk: 8 (over z, core).
Axes of the slice: x: 2, y: 2, z: 4, core: 2. Of those that a mesh axis runs over, the one named last changes fastest.
Arguments:
- hyper_state: float32 [32, 4, 2048], P(('req', 'blk')), may hold values from -6 to 6
- lengths: int32 [32], P('req'), may hold values from 1 to 16384
- key_cache: bfloat16 [32, 16, 2052, 128], P('req', 'blk'), may hold values from -360 to 360
- value_cache: bfloat16 [32, 16, 2052, 128], P('req', 'blk'), may hold values from -6 to 6
- attn_in_weight: bfloat16 [3, 2048, 2048], P(None, None, 'blk'), may hold values from -0.125 to 0.125
- attn_out_weight: bfloat16 [2048, 2048], P('blk'), may hold values from -0.125 to 0.125
- w_gate: bfloat16 [2048, 8192], P('req', 'blk'), may hold values from -0.125 to 0.125
- w_up: bfloat16 [2048, 8192], P('req', 'blk'), may hold values from -0.125 to 0.125
- w_down: bfloat16 [8192, 2048], P('blk', 'req'), may hold values from -0.0625 to 0.0625
- width_in: float32 [2, 4], replicated, may hold values from 0.2 to 1
- stream_mix: float32 [2, 4, 4], replicated, may hold values from -0.6 to 0.6
- depth_out: float32 [2, 4], replicated, may hold values from 0.5 to 1.5
Outputs:
- hyper_out: float32 [32, 4, 2048], P(('req', 'blk'))
All inputs are finite; a program needn't handle non-finite values.
Results may differ from a plain program's by a relative error of at most 0.023.
Values may be sent and summed in bfloat16 or wider, within the bound.
A program may use at most 128 MiB of HBM per device.

v0:
```python
import math

import jax
import jax.numpy as jnp
from jax import lax
from jax.sharding import PartitionSpec as P


def layer_norm(values):
    center = values - jnp.mean(values, axis=-1, keepdims=True)
    spread = jnp.mean(center * center, axis=-1, keepdims=True)
    return center * lax.rsqrt(spread + 1e-05)


def combine(state, weights):
    return jnp.sum(state * weights[None, :, None], axis=1)


def remix(state, matrix):
    return jnp.sum(state[:, :, None, :] * matrix[None, :, :, None], axis=1)


def rotate(values, positions):
    half = values.shape[-1] // 2
    index = jnp.arange(half).astype(jnp.float32)
    freqs = jnp.exp(index * (-2.0 * math.log(10000.0) / values.shape[-1]))
    angles = positions.astype(jnp.float32)[:, None, None] * freqs[None, None, :]
    cosine = jnp.cos(angles)
    sine = jnp.sin(angles)
    first = values[..., :half]
    second = values[..., half:]
    return jnp.concatenate(
        [first * cosine - second * sine, second * cosine + first * sine], axis=-1
    )


def attend_group(query, key_new, value_new, keys, values, lengths):
    scale = query.shape[-1] ** (-0.5)
    scores = jnp.einsum("rhe,rhse->rhs", query, keys, preferred_element_type=jnp.float32) * scale
    own = jnp.sum(query.astype(jnp.float32) * key_new.astype(jnp.float32), axis=-1) * scale
    valid = jnp.arange(keys.shape[2])[None, None, :] < lengths[:, None, None]
    peak = jnp.maximum(jnp.max(jnp.where(valid, scores, -jnp.inf), axis=-1), own)
    shares = jnp.where(valid, jnp.exp(scores - peak[..., None]), 0.0)
    own_share = jnp.exp(own - peak)
    denom = jnp.sum(shares, axis=-1) + own_share
    probs = (shares / denom[..., None]).astype(jnp.bfloat16)
    own_prob = (own_share / denom).astype(jnp.bfloat16)
    mixed = jnp.einsum("rhs,rhse->rhe", probs, values, preferred_element_type=jnp.float32)
    mixed = mixed + own_prob.astype(jnp.float32)[..., None] * value_new.astype(jnp.float32)
    return mixed.astype(jnp.bfloat16)


def on_device(
    hyper_state,
    lengths,
    key_cache,
    value_cache,
    attn_in_weight,
    attn_out_weight,
    w_gate,
    w_up,
    w_down,
    width_in,
    stream_mix,
    depth_out,
):
    rows_here = hyper_state.shape[0]
    heads_here = key_cache.shape[1]
    head_size = key_cache.shape[3]
    normed = layer_norm(combine(hyper_state, width_in[0])).astype(jnp.bfloat16)
    projected = jnp.einsum(
        "rd,kde->rke",
        lax.all_gather(normed, "blk", axis=0, tiled=True),
        attn_in_weight,
        preferred_element_type=jnp.float32,
    )
    group = projected.shape[0]
    query = rotate(projected[:, 0].reshape(group, heads_here, head_size), lengths).astype(
        jnp.bfloat16
    )
    key_new = rotate(projected[:, 1].reshape(group, heads_here, head_size), lengths).astype(
        jnp.bfloat16
    )
    value_new = projected[:, 2].reshape(group, heads_here, head_size).astype(jnp.bfloat16)
    attended = attend_group(query, key_new, value_new, key_cache, value_cache, lengths)
    flat = attended.reshape(group, heads_here * head_size)
    attn_out = lax.psum_scatter(
        jnp.dot(flat, attn_out_weight, preferred_element_type=jnp.float32),
        "blk",
        scatter_dimension=0,
        tiled=True,
    )
    state = remix(hyper_state, stream_mix[0]) + depth_out[0][None, :, None] * attn_out[:, None, :]
    normed_mlp = layer_norm(combine(state, width_in[1])).astype(jnp.bfloat16)
    everyone = lax.all_gather(normed_mlp, ("req", "blk"), axis=0, tiled=True)
    feature_part = w_gate.shape[0]
    columns = lax.dynamic_slice_in_dim(
        everyone, lax.axis_index("req") * feature_part, feature_part, 1
    )
    gate_part = jnp.dot(columns, w_gate, preferred_element_type=jnp.float32)
    upward_part = jnp.dot(columns, w_up, preferred_element_type=jnp.float32)
    gate, upward = (
        lax.psum_scatter(gate_part, "req", scatter_dimension=0, tiled=True),
        lax.psum_scatter(upward_part, "req", scatter_dimension=0, tiled=True),
    )
    hidden = (jax.nn.silu(gate) * upward).astype(jnp.bfloat16)
    hidden_all = lax.all_gather(hidden, "req", axis=0, tiled=True)
    down_cols = jnp.dot(hidden_all, w_down, preferred_element_type=jnp.float32)
    req_count = lax.axis_size("req")
    blk_count = lax.axis_size("blk")
    column_part = w_down.shape[1]
    ordered = down_cols.reshape(req_count, blk_count, rows_here, column_part)
    ordered = jnp.transpose(ordered, (1, 0, 2, 3)).reshape(
        blk_count * req_count * rows_here, column_part
    )
    summed = lax.psum_scatter(ordered, "blk", scatter_dimension=0, tiled=True)
    mlp_out = lax.all_to_all(summed, "req", split_axis=0, concat_axis=1, tiled=True)
    return remix(state, stream_mix[1]) + depth_out[1][None, :, None] * mlp_out[:, None, :]


def solution(mesh):
    placed = (
        P(("req", "blk"), None, None),
        P("req"),
        P("req", "blk", None, None),
        P("req", "blk", None, None),
        P(None, None, "blk"),
        P("blk", None),
        P("req", "blk"),
        P("req", "blk"),
        P("blk", "req"),
        P(),
        P(),
        P(),
    )
    return jax.shard_map(
        on_device,
        mesh=mesh,
        in_specs=placed,
        out_specs=P(("req", "blk"), None, None),
        check_vma=False,
    )
```

profile of v0, /device:TPU:0, one launch (start us, length us, event | category | flops | bytes accessed | tf_op | source)
XLA Modules:
  0.0 263.4 jit_solution(7520860728214551712)
XLA Ops:
  6.5 0.8 convert_element_type.81
  7.4 0.9 iota_compare_fusion
  8.2 0.8 slice_bitcast_fusion.4
  9.0 1.5 multiply_reduce_fusion.2
  11.1 0.6 multiply_reduce_fusion.6
  12.4 15.7 %all-gather = bf16[16384]{0:T(1024)(128)(2,1)S(1)} all-gather(bf16[2048]{0:T(1024)(128)(2,1)S(1)} %multiply_convert_fusion.1), channel_id=2, replica_groups=mesh['req'=4,'blk'=8] {'blk'}, dimensions={0}, use_global_device_ids=true | all-gather | bytes 36864 | tf_op jit(solution)/shard_map/all_gather | solution.py:73
  28.1 0.5 fusion.29
  28.7 0.1 multiply_cosine_fusion
  28.8 0.1 subtract_convert_fusion
  28.9 0.1 fusion.24
  28.9 0.2 multiply_reduce_fusion.5
  29.1 6.1 %fusion.2 = f32[8,2,1,2052]{3,2,1,0:T(1,128)S(1)} fusion(bf16[8,2,2052,128]{3,1,2,0:T(2,128)(2,1)} %param.14, bf16[8,2,128,1]{2,0,1,3:T(8,128)(2,1)S(1)} %fusion.24), kind=kOutput, calls=%fused_computation.2 | convolution fusion | flops 8404992 | bytes 8540416 | tf_op jit(solution)/shard_map/rhe,rhse->rhs/dot_general | solution.py:39
  35.2 0.1 select_reduce_fusion
  35.3 0.2 fusion.5
  35.5 0.1 fusion.6
  35.7 0.0 copy-start.6
  35.7 1.7 fusion
  37.4 0.9 fusion.19
  38.4 0.0 all-reduce.9.cloned.1.call-update
  38.4 0.0 all-reduce.13.cloned.1.call-start
  38.5 0.1 multiply_reduce_fusion.1
  38.6 0.6 dynamic-slice
  39.2 54.0 %all-reduce.9.cloned.1.call-done = f32[8,2048]{1,0:T(8,128)} async-done(((f32[8,2048]{1,0:T(8,128)}), f32[8,2048]{1,0:T(8,128)}) %all-reduce.9.cloned.1.call-update) | async-done | bytes 65552
  93.2 1.5 constant_dynamic-slice_fusion
  94.7 0.8 fusion.13
  96.1 0.7 multiply_reduce_fusion.4
  97.5 40.0 %all-gather.1 = bf16[65536]{0:T(1024)(128)(2,1)S(1)} all-gather(bf16[2048]{0:T(1024)(128)(2,1)S(1)} %multiply_convert_fusion), channel_id=3, replica_groups=mesh['req'=4,'blk'=8] {'req','blk'}, dimensions={0}, use_global_device_ids=true | all-gather | bytes 135168 | tf_op jit(solution)/shard_map/all_gather | solution.py:95
  137.6 0.1 reshape.434
  137.6 2.2 fusion.9
  139.8 2.2 fusion.11
  142.0 0.0 all-reduce.13.cloned.1.call-update
  142.0 0.0 all-reduce.11.cloned.1.call-start
  142.1 0.7 dynamic-slice.2
  144.1 37.5 %all-reduce.13.cloned.1.call-done = (f32[32,1024]{1,0:T(8,128)}, f32[32,1024]{1,0:T(8,128)}) async-done(((f32[32,1024]{1,0:T(8,128)}, f32[32,1024]{1,0:T(8,128)}), (f32[32,1024]{1,0:T(8,128)}, f32[32,1024]{1,0:T(8,128)})) %all-reduce.13.cloned.1.call-update) | async-done | bytes 262160
  181.5 0.8 fusion.7
  182.3 8.2 %all_gather.11 = bf16[32,1024]{1,0:T(8,128)(2,1)S(1)} all-gather(bf16[8,1024]{1,0:T(8,128)(2,1)S(1)} %fusion.7), channel_id=1, replica_groups=mesh['req'=4,'blk'=8] {'req'}, dimensions={0}, use_global_device_ids=true | all-gather | bytes 81920 | tf_op jit(solution)/shard_map/all_gather | solution.py:107
  190.5 1.5 convolution_bitcast_fusion
  192.0 0.1 copy.54
  192.1 0.6 reshape.431
  192.7 0.0 all-reduce.11.cloned.1.call-update
  192.8 0.1 multiply_add_fusion
  192.8 53.7 %all-reduce.11.cloned.1.call-done = f32[32,512]{1,0:T(8,128)} async-done(((f32[32,512]{1,0:T(8,128)}), f32[32,512]{1,0:T(8,128)}) %all-reduce.11.cloned.1.call-update) | async-done | bytes 65552
  246.5 0.7 dynamic-slice_bitcast_fusion
  247.2 0.6 copy.23
  247.8 3.6 %all-to-all-start = ((f32[4,1,512]{2,1,0:T(1,128)}), f32[4,1,512]{2,1,0:T(1,128)S(1)}, u32[]{:S(2)}, u32[]{:S(2)}) async-start(f32[4,1,512]{2,1,0:T(1,128)} %copy.23), calls=%async_computation | async-start | bytes 16384 | tf_op jit(solution)/shard_map/all_to_all | solution.py:117
  251.5 0.1 multiply_reduce_fusion
  251.6 4.6 %all-to-all-done = f32[4,1,512]{2,1,0:T(1,128)S(1)} async-done(((f32[4,1,512]{2,1,0:T(1,128)}), f32[4,1,512]{2,1,0:T(1,128)S(1)}, u32[]{:S(2)}, u32[]{:S(2)}) %all-to-all-start) | async-done | bytes 8224 | tf_op jit(solution)/shard_map/all_to_all | solution.py:117
  256.2 0.7 bitcast_add_fusion.1
  (22 shorter events, 0.1 us)
Async XLA Ops:
  6.5 21.6 %copy-start = (bf16[3,2048,256]{2,1,0:T(8,128)(2,1)S(1)}, bf16[3,2048,256]{2,1,0:T(8,128)(2,1)}, u32[]{:S(2)}) copy-start(bf16[3,2048,256]{2,1,0:T(8,128)(2,1)} %param.16) | copy-start | bytes 9437188
  6.5 86.6 %all-reduce.9.cloned.1.call-start = ((), (), s32[]{:S(2)}) async-start(), calls=%async_computation.1 | async-start | bytes 131072
  28.1 7.5 %copy-start.4 = (bf16[8,2,2052,128]{3,1,2,0:T(2,128)(2,1)S(1)}, bf16[8,2,2052,128]{3,1,2,0:T(2,128)(2,1)}, u32[]{:S(2)}) copy-start(bf16[8,2,2052,128]{3,1,2,0:T(2,128)(2,1)} %param.15) | copy-start | bytes 25214980
  35.2 2.3 copy-start.1
  35.6 2.8 %copy-start.3 = (f32[2,4,4]{2,1,0:T(4,128)S(1)}, f32[2,4,4]{2,1,0:T(4,128)}, u32[]{:S(2)}) copy-start(f32[2,4,4]{2,1,0:T(4,128)} %param.22) | copy-start | bytes 388
  35.7 2.8 %copy-start.2 = (f32[1,4,2048]{2,1,0:T(4,128)S(1)}, f32[1,4,2048]{2,1,0:T(4,128)}, u32[]{:S(2)}) copy-start(f32[1,4,2048]{2,1,0:T(4,128)} %param.12) | copy-start | bytes 98308
  35.7 2.9 %copy-start.6 = (u32[32]{0:T(128)S(1)}, u32[32]{0:T(128)}, u32[]{:S(2)}) copy-start(u32[32]{0:T(128)} %constant.42) | copy-start | bytes 388
  35.7 106.4 %copy-start.5 = (u32[32]{0:T(128)S(1)}, u32[32]{0:T(128)}, u32[]{:S(2)}) copy-start(u32[32]{0:T(128)} %constant.46) | copy-start | bytes 388
  38.4 143.2 %all-reduce.13.cloned.1.call-start = ((), (), s32[]{:S(2)}) async-start(), calls=%async_computation.3 | async-start | bytes 524288
  142.0 104.5 %all-reduce.11.cloned.1.call-start = ((), (), s32[]{:S(2)}) async-start(), calls=%async_computation.2 | async-start | bytes 131072
  247.8 8.3 %all-to-all-start = ((f32[4,1,512]{2,1,0:T(1,128)}), f32[4,1,512]{2,1,0:T(1,128)S(1)}, u32[]{:S(2)}, u32[]{:S(2)}) async-start(f32[4,1,512]{2,1,0:T(1,128)} %copy.23), calls=%async_computation | async-start | bytes 16384 | tf_op jit(solution)/shard_map/all_to_all | solution.py:117
Sparse Core Ops, SparseCore 0:
  38.5 54.6 all-reduce.8
  142.1 39.3 all-reduce.12
  192.9 53.5 all-reduce.10
where the time goes:
time: 264 us; the launch traced here: 263 us
  waiting for transfers between devices  150 us (57%)
  blocking collectives  63.9 us (24%)
  between operations  17.4 us (7%)
  matrix products  15.1 us (6%)
  other arithmetic  7.85 us (3%)
  local copies, waits for them, and re-layouts  5.67 us (2%)
  starting transfers between devices  3.73 us (1%)
    unnamed x6, waiting for transfers between devices  145 us
    all_gather x1, blocking collectives, on_device(): everyone = lax.all_gather(normed_mlp, ('req', 'blk'), axis=0, tiled=True)  40 us
    all_gather x1, blocking collectives, on_device(): lax.all_gather(normed, 'blk', axis=0, tiled=True)  15.7 us
    all_gather x1, blocking collectives, on_device(): hidden_all = lax.all_gather(hidden, 'req', axis=0, tiled=True)  8.18 us
    dot_general x1, matrix products, attend_group(): jnp.einsum('rhe,rhse->rhs', query, keys, preferred_element_type=jnp.float32)  6.08 us
  transfers between devices with their start and end apart: 4, of which 4 were waited for; matrix products, arithmetic and copies ran while one was open for 1% of the time, Pallas kernels for 0%

commit v1 on v0

v1 whole, which is shorter than its diff:
```python
import functools
import math

import jax
import jax.numpy as jnp
import numpy as np
from jax import lax
from jax.experimental import pallas as pl
from jax.experimental.pallas import tpu as pltpu
from jax.sharding import PartitionSpec as P

MESH = pl.DeviceIdType.MESH
LANES = 128
F32 = jnp.float32
BF16 = jnp.bfloat16


def split_two_pi():
    whole = 2.0 * math.pi
    one = float(np.round(whole * 2.0**8) / 2.0**8)
    two = float(np.round((whole - one) * 2.0**20) / 2.0**20)
    return one, two, whole - one - two


def sine_cosine(angles):
    one, two, three = split_two_pi()
    turns = jnp.floor(angles * (1.0 / (2.0 * math.pi)) + 0.5)
    rest = ((angles - turns * one) - turns * two) - turns * three
    return jnp.sin(rest), jnp.cos(rest)


def normalize(row):
    count = row.shape[0] * row.shape[1]
    center = row - jnp.sum(row, keepdims=True) * (1.0 / count)
    spread = jnp.sum(center * center, keepdims=True) * (1.0 / count)
    return center * lax.rsqrt(spread + 1e-05)


def gather_lanes(ref):
    return jnp.concatenate([ref[:, k, :] for k in range(ref.shape[1])], axis=1)


def scatter_lanes(ref, values):
    for k in range(ref.shape[1]):
        ref[:, k, :] = values[:, k * LANES : (k + 1) * LANES]


def wait_bytes(ref, sem):
    pltpu.make_async_copy(ref, ref, sem).wait()


def layer_kernel(
    req_count,
    blk_count,
    hyper_ref,
    lengths_ref,
    freq_ref,
    width_ref,
    mix_ref,
    depth_ref,
    keys_hbm,
    values_hbm,
    win_hbm,
    wout_hbm,
    wgate_hbm,
    wup_hbm,
    wdown_hbm,
    out_ref,
    keys,
    values,
    win,
    wout,
    wgate,
    wup,
    wdown,
    streams,
    row_send,
    row_recv,
    attn_send,
    attn_recv,
    norm_send,
    norm_recv,
    gate_send,
    gate_recv,
    hid_send,
    hid_recv,
    down_send,
    down_recv,
    mlp_row,
    load_sem,
    key_sem,
    value_sem,
    blk_send_sem,
    blk_recv_sem,
    req_send_sem,
    req_recv_sem,
    all_send_sem,
    all_recv_sem,
):
    req = lax.axis_index("req")
    blk = lax.axis_index("blk")
    everyone = req_count * blk_count
    me = req * blk_count + blk
    group, heads, slots, head = keys.shape

    loads = [pltpu.make_async_copy(win_hbm.at[k], win.at[k], load_sem.at[k]) for k in range(3)]
    key_loads = [
        pltpu.make_async_copy(keys_hbm.at[r], keys.at[r], key_sem.at[r]) for r in range(group)
    ]
    value_loads = [
        pltpu.make_async_copy(values_hbm.at[r], values.at[r], value_sem.at[r])
        for r in range(group)
    ]
    late = [
        pltpu.make_async_copy(src, dst, load_sem.at[3 + i])
        for i, (src, dst) in enumerate(
            [(wout_hbm, wout), (wgate_hbm, wgate), (wup_hbm, wup), (wdown_hbm, wdown)]
        )
    ]
    barrier = pltpu.get_barrier_semaphore()

    def greet(i, carry):
        other = lax.rem(me + i, everyone)
        pl.semaphore_signal(
            barrier,
            inc=1,
            device_id=(other // blk_count, lax.rem(other, blk_count)),
            device_id_type=MESH,
        )
        return carry

    lax.fori_loop(1, everyone, greet, 0)
    for copy in loads + key_loads + value_loads + late:
        copy.start()

    for k in range(streams.shape[1]):
        streams[:, k, :] = hyper_ref[0, :, k * LANES : (k + 1) * LANES]
    count = streams.shape[0]
    state = [streams[s] for s in range(count)]
    row = functools.reduce(lambda a, b: a + b, [state[s] * width_ref[0, s] for s in range(count)])
    row_send[...] = normalize(row)

    pl.semaphore_wait(barrier, everyone - 1)

    def blk_exchange(phase, source_of, landing):
        copies = []
        for d in range(1, blk_count):
            other = lax.rem(blk + d, blk_count)
            copy = pltpu.make_async_remote_copy(
                src_ref=source_of(other),
                dst_ref=landing.at[blk],
                send_sem=blk_send_sem.at[phase, d - 1],
                recv_sem=blk_recv_sem.at[phase, d - 1],
                device_id=(req, other),
                device_id_type=MESH,
            )
            copy.start()
            copies.append(copy)
        return copies

    def blk_arrivals(phase, source_of, landing):
        for d in range(1, blk_count):
            other = lax.rem(blk + blk_count - d, blk_count)
            pltpu.make_async_remote_copy(
                src_ref=source_of(other),
                dst_ref=landing.at[other],
                send_sem=blk_send_sem.at[phase, d - 1],
                recv_sem=blk_recv_sem.at[phase, d - 1],
                device_id=(req, other),
                device_id_type=MESH,
            ).wait_recv()

    def req_exchange(phase, source_of, landing):
        copies = []
        for d in range(1, req_count):
            other = lax.rem(req + d, req_count)
            copy = pltpu.make_async_remote_copy(
                src_ref=source_of(other),
                dst_ref=landing.at[req],
                send_sem=req_send_sem.at[phase, d - 1],
                recv_sem=req_recv_sem.at[phase, d - 1],
                device_id=(other, blk),
                device_id_type=MESH,
            )
            copy.start()
            copies.append(copy)
        return copies

    def req_arrivals(phase, source_of, landing):
        for d in range(1, req_count):
            other = lax.rem(req + req_count - d, req_count)
            pltpu.make_async_remote_copy(
                src_ref=source_of(other),
                dst_ref=landing.at[other],
                send_sem=req_send_sem.at[phase, d - 1],
                recv_sem=req_recv_sem.at[phase, d - 1],
                device_id=(other, blk),
                device_id_type=MESH,
            ).wait_recv()

    def all_exchange(phase, source_of, landing):
        def send(i, carry):
            other = lax.rem(me + i, everyone)
            other_req = other // blk_count
            pltpu.make_async_remote_copy(
                src_ref=source_of(other, other_req),
                dst_ref=landing.at[me],
                send_sem=all_send_sem.at[phase],
                recv_sem=all_recv_sem.at[phase],
                device_id=(other_req, lax.rem(other, blk_count)),
                device_id_type=MESH,
            ).start()
            return carry

        lax.fori_loop(1, everyone, send, 0)

    def finish(copies):
        for copy in copies:
            copy.wait_send()

    row_copies = blk_exchange(0, lambda other: row_send, row_recv)
    row_recv[blk] = row_send[...]

    row_at = lax.broadcasted_iota(jnp.int32, (group, 1), 0)
    lengths = jnp.zeros((group, 1), jnp.int32)
    for r in range(group):
        lengths = jnp.where(row_at == r, lengths_ref[r], lengths)
    angles = lengths.astype(F32) * freq_ref[...]
    sine, cosine = sine_cosine(angles)
    lane = lax.broadcasted_iota(jnp.int32, (group, head), 1)
    sine = jnp.where(lane < head // 2, -sine, sine)

    def rotate(part):
        return (part * cosine + pltpu.roll(part, head // 2, 1) * sine).astype(BF16)

    mixed_state = [
        functools.reduce(lambda a, b: a + b, [state[s] * mix_ref[0, s, t] for s in range(count)])
        for t in range(count)
    ]

    blk_arrivals(0, lambda other: row_send, row_recv)
    normed = gather_lanes(row_recv).astype(BF16)
    projected = []
    for k in range(3):
        loads[k].wait()
        projected.append(jnp.dot(normed, win[k], preferred_element_type=F32))
    finish(row_copies)

    scale = head ** (-0.5)
    heads_of = [slice(h * head, (h + 1) * head) for h in range(heads)]
    query = [rotate(projected[0][:, part]) for part in heads_of]
    key_new = [rotate(projected[1][:, part]) for part in heads_of]
    value_new = [projected[2][:, part].astype(BF16).astype(F32) for part in heads_of]
    scores = [None] * heads
    for r in range(group):
        key_loads[r].wait()
        for h in range(heads):
            part = lax.dot_general(
                query[h], keys[r, h], (((1,), (1,)), ((), ())), preferred_element_type=F32
            )
            scores[h] = part if r == 0 else jnp.where(row_at == r, part, scores[h])
    slot = lax.broadcasted_iota(jnp.int32, (group, slots), 1)
    shares, own_share, denom = [], [], []
    for h in range(heads):
        own = scale * jnp.sum(
            query[h].astype(F32) * key_new[h].astype(F32), axis=-1, keepdims=True
        )
        masked = jnp.where(slot < lengths, scores[h] * scale, -jnp.inf)
        peak = jnp.maximum(jnp.max(masked, axis=-1, keepdims=True), own)
        share = jnp.exp(masked - peak)
        own_share.append(jnp.exp(own - peak))
        denom.append(jnp.sum(share, axis=-1, keepdims=True) + own_share[h])
        shares.append(share.astype(BF16))
    mixed = [None] * heads
    for r in range(group):
        value_loads[r].wait()
        for h in range(heads):
            part = jnp.dot(shares[h], values[r, h], preferred_element_type=F32)
            mixed[h] = part if r == 0 else jnp.where(row_at == r, part, mixed[h])
    flat = jnp.concatenate(
        [(mixed[h] + own_share[h] * value_new[h]) / denom[h] for h in range(heads)], axis=1
    ).astype(BF16)
    late[0].wait()
    scatter_lanes(attn_send, jnp.dot(flat, wout[...], preferred_element_type=F32))

    attn_copies = blk_exchange(1, lambda other: attn_send.at[other], attn_recv)
    attn_recv[blk] = attn_send[blk]
    blk_arrivals(1, lambda other: attn_send.at[other], attn_recv)
    attn_out = functools.reduce(lambda a, b: a + b, [attn_recv[j] for j in range(blk_count)])
    state = [mixed_state[t] + depth_ref[0, t] * attn_out for t in range(count)]
    row = functools.reduce(lambda a, b: a + b, [state[s] * width_ref[1, s] for s in range(count)])
    row = normalize(row)
    chunk = norm_send.shape[1]
    for c in range(req_count):
        norm_send[c] = row[c * chunk : (c + 1) * chunk]

    all_exchange(0, lambda other, other_req: norm_send.at[other_req], norm_recv)
    norm_recv[me] = norm_send[req]
    finish(attn_copies)
    mixed_state = [
        functools.reduce(lambda a, b: a + b, [state[s] * mix_ref[1, s, t] for s in range(count)])
        for t in range(count)
    ]
    others = pl.ds(0, everyone - 1)
    late[1].wait()
    late[2].wait()
    wait_bytes(norm_recv.at[others], all_recv_sem.at[0])
    columns = gather_lanes(norm_recv).astype(BF16)
    gate = jnp.dot(columns, wgate[...], preferred_element_type=F32)
    up = jnp.dot(columns, wup[...], preferred_element_type=F32)
    for c in range(req_count):
        rows = slice(c * group, (c + 1) * group)
        gate_send[c] = jnp.concatenate([gate[rows], up[rows]], axis=0).astype(BF16)

    gate_copies = req_exchange(0, lambda other: gate_send.at[other], gate_recv)
    gate_recv[req] = gate_send[req]
    wait_bytes(norm_recv.at[others], all_send_sem.at[0])
    req_arrivals(0, lambda other: gate_send.at[other], gate_recv)
    both = functools.reduce(
        lambda a, b: a + b, [gate_recv[c].astype(F32) for c in range(req_count)]
    )
    gate, up = both[:group], both[group:]
    hidden = gate / (1.0 + jnp.exp(-gate)) * up
    half = hidden.shape[1] // 2
    hid_send[...] = jnp.concatenate([hidden[:, :half], hidden[:, half:]], axis=0).astype(BF16)

    hid_copies = req_exchange(1, lambda other: hid_send, hid_recv)
    hid_recv[req] = hid_send[...]
    finish(gate_copies)
    late[3].wait()
    req_arrivals(1, lambda other: hid_send, hid_recv)
    stacked = hid_recv[...].reshape(req_count * 2 * group, half)
    first = jnp.dot(stacked, wdown[:half], preferred_element_type=F32)
    second = jnp.dot(stacked, wdown[half:], preferred_element_type=F32)
    for c in range(req_count):
        low = 2 * group * c
        part = first[low : low + group] + second[low + group : low + 2 * group]
        scatter_lanes(down_send.at[pl.ds(c * group, group)], part)

    all_exchange(1, lambda other, other_req: down_send.at[other], down_recv)
    down_recv[me] = down_send[me]
    finish(hid_copies)
    wait_bytes(down_recv.at[others], all_recv_sem.at[1])
    for c in range(req_count):
        mlp_row[c * chunk : (c + 1) * chunk] = functools.reduce(
            lambda a, b: a + b, [down_recv[c * blk_count + j] for j in range(blk_count)]
        )
    mlp_out = mlp_row[...]
    for t in range(count):
        streams[t] = mixed_state[t] + depth_ref[1, t] * mlp_out
    for k in range(streams.shape[1]):
        out_ref[0, :, k * LANES : (k + 1) * LANES] = streams[:, k, :]
    wait_bytes(down_recv.at[others], all_send_sem.at[1])


def on_device(
    hyper_state,
    lengths,
    key_cache,
    value_cache,
    attn_in_weight,
    attn_out_weight,
    w_gate,
    w_up,
    w_down,
    width_in,
    stream_mix,
    depth_out,
):
    req_count = lax.axis_size("req")
    blk_count = lax.axis_size("blk")
    everyone = req_count * blk_count
    _, count, width = hyper_state.shape
    group, _, _, head = key_cache.shape
    feature_part, hid_part = w_gate.shape
    parts = width // LANES
    chunk = feature_part // LANES
    freqs = np.exp(np.arange(head // 2) * (-2.0 * math.log(10000.0) / head))
    freqs = np.concatenate([freqs, freqs]).astype(np.float32)[None, :]
    vmem = pl.BlockSpec(memory_space=pltpu.VMEM)
    smem = pl.BlockSpec(memory_space=pltpu.SMEM)
    hbm = pl.BlockSpec(memory_space=pl.ANY)
    like = lambda x: pltpu.VMEM(x.shape, x.dtype)
    dma = pltpu.SemaphoreType.DMA
    big = [key_cache, value_cache, attn_in_weight, attn_out_weight, w_gate, w_up, w_down]
    return pl.pallas_call(
        functools.partial(layer_kernel, req_count, blk_count),
        out_shape=jax.ShapeDtypeStruct(hyper_state.shape, hyper_state.dtype),
        in_specs=[vmem, smem, vmem, smem, smem, smem] + [hbm] * len(big),
        out_specs=vmem,
        scratch_shapes=[like(x) for x in big]
        + [
            pltpu.VMEM((count, parts, LANES), F32),
            pltpu.VMEM((parts, LANES), F32),
            pltpu.VMEM((blk_count, parts, LANES), F32),
            pltpu.VMEM((blk_count, parts, LANES), F32),
            pltpu.VMEM((blk_count, parts, LANES), F32),
            pltpu.VMEM((req_count, chunk, LANES), F32),
            pltpu.VMEM((everyone, chunk, LANES), F32),
            pltpu.VMEM((req_count, 2 * group, hid_part), BF16),
            pltpu.VMEM((req_count, 2 * group, hid_part), BF16),
            pltpu.VMEM((2 * group, hid_part // 2), BF16),
            pltpu.VMEM((req_count, 2 * group, hid_part // 2), BF16),
            pltpu.VMEM((everyone, chunk, LANES), F32),
            pltpu.VMEM((everyone, chunk, LANES), F32),
            pltpu.VMEM((parts, LANES), F32),
            dma((7,)),
            dma((group,)),
            dma((group,)),
            dma((2, blk_count - 1)),
            dma((2, blk_count - 1)),
            dma((2, req_count - 1)),
            dma((2, req_count - 1)),
            dma((2,)),
            dma((2,)),
        ],
        compiler_params=pltpu.CompilerParams(
            collective_id=0, has_side_effects=True, vmem_limit_bytes=56 * 2**20
        ),
        name="layer_step",
    )(hyper_state, lengths, jnp.asarray(freqs), width_in, stream_mix, depth_out, *big)


def solution(mesh):
    placed = (
        P(("req", "blk"), None, None),
        P("req"),
        P("req", "blk", None, None),
        P("req", "blk", None, None),
        P(None, None, "blk"),
        P("blk", None),
        P("req", "blk"),
        P("req", "blk"),
        P("blk", "req"),
        P(),
        P(),
        P(),
    )
    return jax.shard_map(
        on_device,
        mesh=mesh,
        in_specs=placed,
        out_specs=P(("req", "blk"), None, None),
        check_vma=False,
    )
```

time: 264 us -> 58.1 us (0.22)
  waiting for transfers between devices: 150 us -> 0 us
  blocking collectives: 63.9 us -> 0 us
  Pallas kernels: 0 us -> 41 us
  between operations: 17.4 us -> 0.01 us
  matrix products: 15.1 us -> 0 us
  local copies, waits for them, and re-layouts: 5.67 us -> 16.8 us
  other arithmetic: 7.85 us -> 0 us
  starting transfers between devices: 3.73 us -> 0 us
    unnamed x6 -> x0, waiting for transfers between devices: 145 us -> none
    all_gather x3 -> x0, blocking collectives: 63.9 us -> none  [the longest x1 40 us: on_device(): everyone = lax.all_gather(normed_mlp, ('req', 'blk'), axis=0, tiled=True)]
    pallas_call x0 -> x1, Pallas kernels: none -> 41 us  [on_device(): pl.pallas_call(functools.partial(layer_kernel, req_count, blk_count), out...]
    dot_general x7 -> x0, matrix products: 15.1 us -> none  [the longest x1 6.08 us: attend_group(): jnp.einsum('rhe,rhse->rhs', query, keys, preferred_element_type=jnp.float32)]
    unnamed x17 -> x3, local copies, waits for them, and re-layouts: 2.79 us -> 16.8 us
    all_to_all x1 -> x0, waiting for transfers between devices: 4.59 us -> none  [on_device(): lax.all_to_all(summed, 'req', split_axis=0, concat_axis=1, tiled=True)]
    reduce_sum x8 -> x0, other arithmetic: 4.06 us -> none  [the longest x2 2.22 us: layer_norm(): center = values - jnp.mean(values, axis=-1, keepdims=True)]
    all_to_all x1 -> x0, starting transfers between devices: 3.65 us -> none  [on_device(): lax.all_to_all(summed, 'req', split_axis=0, concat_axis=1, tiled=True)]
  transfers between devices with their start and end apart: 4 -> 0, of which waited for: 4 -> 0; matrix products, arithmetic and copies ran while one was open for 1% -> 0% of each run, Pallas kernels for 0% -> 0%
where the time goes in v1:
time: 58.1 us; the launch traced here: 57.8 us
  Pallas kernels  41 us (71%)
  local copies, waits for them, and re-layouts  16.8 us (29%)
    pallas_call x1, Pallas kernels, on_device(): pl.pallas_call(functools.partial(layer_kernel, req_count, blk_count), out...  41 us
    unnamed x3, local copies, waits for them, and re-layouts  16.8 us

profile of v1, /device:TPU:0, one launch (start us, length us, event | category | flops | bytes accessed | tf_op | source)
XLA Modules:
  0.0 57.8 jit_solution(8940482821096145514)
XLA Ops:
  0.0 7.7 %copy.14.keys_hbm = bf16[8,2,2052,128]{3,2,1,0:T(8,128)(2,1)} copy(bf16[8,2,2052,128]{3,1,2,0:T(2,128)(2,1)} %param.15) | data formatting | bytes 16809984 | tf_op args[2]
  7.7 7.7 %copy.15.values_hbm = bf16[8,2,2052,128]{3,2,1,0:T(8,128)(2,1)} copy(bf16[8,2,2052,128]{3,1,2,0:T(2,128)(2,1)} %param.16) | data formatting | bytes 16809984 | tf_op args[3]
  15.4 41.0 %layer_step.1 = f32[1,4,2048]{2,1,0:T(4,128)} custom-call(f32[1,4,2048]{2,1,0:T(4,128)} %hyper_ref.1, s32[8]{0:T(128)} %lengths_ref.1, f32[1,128]{1,0:T(1,128)} %constant.2.clone.freq_ref, f32[2,4]{1,0:T(2,128)} %width_ref.1, f32[2,4,4]{2,1,0:T(4,128)} %mix_ref.1, f32[2,4]{1,0:T(2,128)} %depth_ref.1, bf16[8,2,2052,128]{3,2,1,0:T(8,128)(2,1)} %copy.14.keys_hbm, ...), custom_call_target="tpu_custom_call" | custom-call | tf_op jit(solution)/shard_map/layer_step/pallas_call | solution.py:386
  56.4 1.4 %copy.17 = f32[1,4,2048]{2,1,0:T(4,128)} copy(f32[1,4,2048]{2,1,0:T(4,128)} %layer_step.1) | data formatting | bytes 65536

commit v2 on v1

--- a/solution.py
+++ b/solution.py
@@ -101,7 +101,8 @@
     blk = lax.axis_index("blk")
     everyone = req_count * blk_count
     me = req * blk_count + blk
-    group, heads, slots, head = keys.shape
+    group, lines, head = keys.shape
+    heads = win.shape[2] // head
 
     loads = [pltpu.make_async_copy(win_hbm.at[k], win.at[k], load_sem.at[k]) for k in range(3)]
     key_loads = [
@@ -221,13 +222,14 @@
     row_copies = blk_exchange(0, lambda other: row_send, row_recv)
     row_recv[blk] = row_send[...]
 
-    row_at = lax.broadcasted_iota(jnp.int32, (group, 1), 0)
-    lengths = jnp.zeros((group, 1), jnp.int32)
+    row_at = lax.broadcasted_iota(jnp.int32, (heads * group, 1), 0)
+    request_at = lax.rem(row_at, group)
+    lengths = jnp.zeros((heads * group, 1), jnp.int32)
     for r in range(group):
-        lengths = jnp.where(row_at == r, lengths_ref[r], lengths)
+        lengths = jnp.where(request_at == r, lengths_ref[r], lengths)
     angles = lengths.astype(F32) * freq_ref[...]
     sine, cosine = sine_cosine(angles)
-    lane = lax.broadcasted_iota(jnp.int32, (group, head), 1)
+    lane = lax.broadcasted_iota(jnp.int32, (heads * group, head), 1)
     sine = jnp.where(lane < head // 2, -sine, sine)
 
     def rotate(part):
@@ -247,39 +249,37 @@
     finish(row_copies)
 
     scale = head ** (-0.5)
-    heads_of = [slice(h * head, (h + 1) * head) for h in range(heads)]
-    query = [rotate(projected[0][:, part]) for part in heads_of]
-    key_new = [rotate(projected[1][:, part]) for part in heads_of]
-    value_new = [projected[2][:, part].astype(BF16).astype(F32) for part in heads_of]
-    scores = [None] * heads
+
+    def by_head(part):
+        return jnp.concatenate([part[:, h * head : (h + 1) * head] for h in range(heads)], axis=0)
+
+    query = rotate(by_head(projected[0]))
+    key_new = rotate(by_head(projected[1]))
+    value_new = by_head(projected[2]).astype(BF16).astype(F32)
+    own = scale * jnp.sum(query.astype(F32) * key_new.astype(F32), axis=-1, keepdims=True)
     for r in range(group):
         key_loads[r].wait()
-        for h in range(heads):
-            part = lax.dot_general(
-                query[h], keys[r, h], (((1,), (1,)), ((), ())), preferred_element_type=F32
-            )
-            scores[h] = part if r == 0 else jnp.where(row_at == r, part, scores[h])
-    slot = lax.broadcasted_iota(jnp.int32, (group, slots), 1)
-    shares, own_share, denom = [], [], []
-    for h in range(heads):
-        own = scale * jnp.sum(
-            query[h].astype(F32) * key_new[h].astype(F32), axis=-1, keepdims=True
+        part = lax.dot_general(
+            query, keys[r], (((1,), (1,)), ((), ())), preferred_element_type=F32
         )
-        masked = jnp.where(slot < lengths, scores[h] * scale, -jnp.inf)
-        peak = jnp.maximum(jnp.max(masked, axis=-1, keepdims=True), own)
-        share = jnp.exp(masked - peak)
-        own_share.append(jnp.exp(own - peak))
-        denom.append(jnp.sum(share, axis=-1, keepdims=True) + own_share[h])
-        shares.append(share.astype(BF16))
-    mixed = [None] * heads
+        scores = part if r == 0 else jnp.where(request_at == r, part, scores)
+    line = lax.broadcasted_iota(jnp.int32, (heads * group, lines), 1)
+    head_at = row_at // group
+    valid = (line < lengths * heads) & (lax.rem(line, heads) == head_at)
+    scores = jnp.where(valid, scores * scale, -jnp.inf)
+    peak = jnp.maximum(jnp.max(scores, axis=-1, keepdims=True), own)
+    shares = jnp.exp(scores - peak)
+    own_share = jnp.exp(own - peak)
+    denom = jnp.sum(shares, axis=-1, keepdims=True) + own_share
+    shares = shares.astype(BF16)
     for r in range(group):
         value_loads[r].wait()
-        for h in range(heads):
-            part = jnp.dot(shares[h], values[r, h], preferred_element_type=F32)
-            mixed[h] = part if r == 0 else jnp.where(row_at == r, part, mixed[h])
+        part = jnp.dot(shares, values[r], preferred_element_type=F32)
+        mixed = part if r == 0 else jnp.where(request_at == r, part, mixed)
+    mixed = ((mixed + own_share * value_new) / denom).astype(BF16)
     flat = jnp.concatenate(
-        [(mixed[h] + own_share[h] * value_new[h]) / denom[h] for h in range(heads)], axis=1
-    ).astype(BF16)
+        [mixed[h * group : (h + 1) * group] for h in range(heads)], axis=1
+    )
     late[0].wait()
     scatter_lanes(attn_send, jnp.dot(flat, wout[...], preferred_element_type=F32))
 
@@ -371,7 +371,7 @@
     blk_count = lax.axis_size("blk")
     everyone = req_count * blk_count
     _, count, width = hyper_state.shape
-    group, _, _, head = key_cache.shape
+    group, heads, slots, head = key_cache.shape
     feature_part, hid_part = w_gate.shape
     parts = width // LANES
     chunk = feature_part // LANES
@@ -382,7 +382,8 @@
     hbm = pl.BlockSpec(memory_space=pl.ANY)
     like = lambda x: pltpu.VMEM(x.shape, x.dtype)
     dma = pltpu.SemaphoreType.DMA
-    big = [key_cache, value_cache, attn_in_weight, attn_out_weight, w_gate, w_up, w_down]
+    lines = lambda x: jnp.transpose(x, (0, 2, 1, 3)).reshape(group, slots * heads, head)
+    big = [lines(key_cache), lines(value_cache), attn_in_weight, attn_out_weight, w_gate, w_up, w_down]
     return pl.pallas_call(
         functools.partial(layer_kernel, req_count, blk_count),
         out_shape=jax.ShapeDtypeStruct(hyper_state.shape, hyper_state.dtype),

time: 58.1 us -> 42.7 us (0.73)
  local copies, waits for them, and re-layouts: 16.8 us -> 1.38 us
    unnamed x3 -> x1, local copies, waits for them, and re-layouts: 16.8 us -> 1.38 us
where the time goes in v2:
time: 42.7 us; the launch traced here: 42.5 us
  Pallas kernels  41.1 us (96%)
  local copies, waits for them, and re-layouts  1.38 us (3%)
    pallas_call x1, Pallas kernels, on_device(): pl.pallas_call(functools.partial(layer_kernel, req_count, blk_count), out...  41.1 us
    unnamed x1, local copies, waits for them, and re-layouts  1.38 us

profile of v2, /device:TPU:0, one launch (start us, length us, event | category | flops | bytes accessed | tf_op | source)
XLA Modules:
  0.0 42.5 jit_solution(11863913259593582691)
XLA Ops:
  0.0 41.1 %layer_step.1 = f32[1,4,2048]{2,1,0:T(4,128)} custom-call(f32[1,4,2048]{2,1,0:T(4,128)} %hyper_ref.1, s32[8]{0:T(128)} %lengths_ref.1, f32[1,128]{1,0:T(1,128)} %constant.2.clone.freq_ref, f32[2,4]{1,0:T(2,128)} %width_ref.1, f32[2,4,4]{2,1,0:T(4,128)} %mix_ref.1, f32[2,4]{1,0:T(2,128)} %depth_ref.1, bf16[8,4104,128]{2,1,0:T(8,128)(2,1)} %bitcast.6, ...), custom_call_target="tpu_custom_call" | custom-call | tf_op jit(solution)/shard_map/layer_step/pallas_call | solution.py:387
  41.1 1.4 %copy.15 = f32[1,4,2048]{2,1,0:T(4,128)} copy(f32[1,4,2048]{2,1,0:T(4,128)} %layer_step.1) | data formatting | bytes 65536

commit v3 on v2

--- a/solution.py
+++ b/solution.py
@@ -74,6 +74,7 @@
     wup,
     wdown,
     streams,
+    wide_rows,
     row_send,
     row_recv,
     attn_send,
@@ -82,6 +83,8 @@
     norm_recv,
     gate_send,
     gate_recv,
+    up_send,
+    up_recv,
     hid_send,
     hid_recv,
     down_send,
@@ -120,18 +123,16 @@
     ]
     barrier = pltpu.get_barrier_semaphore()
 
-    def greet(i, carry):
-        other = lax.rem(me + i, everyone)
-        pl.semaphore_signal(
-            barrier,
-            inc=1,
-            device_id=(other // blk_count, lax.rem(other, blk_count)),
-            device_id_type=MESH,
-        )
-        return carry
-
-    lax.fori_loop(1, everyone, greet, 0)
-    for copy in loads + key_loads + value_loads + late:
+    reqs = [req] + [lax.rem(req + d, req_count) for d in range(1, req_count)]
+    blks = [blk] + [lax.rem(blk + d, blk_count) for d in range(1, blk_count)]
+    peers = [
+        (reqs[i], blks[j]) for i in range(req_count) for j in range(blk_count) if i + j > 0
+    ]
+    for copy in loads:
+        copy.start()
+    for peer in peers:
+        pl.semaphore_signal(barrier, inc=1, device_id=peer, device_id_type=MESH)
+    for copy in key_loads + value_loads + late:
         copy.start()
 
     for k in range(streams.shape[1]):
@@ -139,81 +140,68 @@
     count = streams.shape[0]
     state = [streams[s] for s in range(count)]
     row = functools.reduce(lambda a, b: a + b, [state[s] * width_ref[0, s] for s in range(count)])
-    row_send[...] = normalize(row)
+    row_send[...] = normalize(row).astype(BF16)
 
     pl.semaphore_wait(barrier, everyone - 1)
 
+    def blk_copy(phase, d, source, landing, slot, other):
+        return pltpu.make_async_remote_copy(
+            src_ref=source,
+            dst_ref=landing.at[slot],
+            send_sem=blk_send_sem.at[phase, d - 1],
+            recv_sem=blk_recv_sem.at[phase, d - 1],
+            device_id=(req, other),
+            device_id_type=MESH,
+        )
+
     def blk_exchange(phase, source_of, landing):
-        copies = []
-        for d in range(1, blk_count):
-            other = lax.rem(blk + d, blk_count)
-            copy = pltpu.make_async_remote_copy(
-                src_ref=source_of(other),
-                dst_ref=landing.at[blk],
-                send_sem=blk_send_sem.at[phase, d - 1],
-                recv_sem=blk_recv_sem.at[phase, d - 1],
-                device_id=(req, other),
-                device_id_type=MESH,
-            )
+        copies = [
+            blk_copy(phase, d, source_of(blks[d]), landing, blk, blks[d])
+            for d in range(1, blk_count)
+        ]
+        for copy in copies:
             copy.start()
-            copies.append(copy)
         return copies
 
     def blk_arrivals(phase, source_of, landing):
         for d in range(1, blk_count):
-            other = lax.rem(blk + blk_count - d, blk_count)
-            pltpu.make_async_remote_copy(
-                src_ref=source_of(other),
-                dst_ref=landing.at[other],
-                send_sem=blk_send_sem.at[phase, d - 1],
-                recv_sem=blk_recv_sem.at[phase, d - 1],
-                device_id=(req, other),
-                device_id_type=MESH,
-            ).wait_recv()
+            other = blks[blk_count - d]
+            blk_copy(phase, d, source_of(other), landing, other, other).wait_recv()
+
+    def req_copy(phase, d, source, landing, slot, other):
+        return pltpu.make_async_remote_copy(
+            src_ref=source,
+            dst_ref=landing.at[slot],
+            send_sem=req_send_sem.at[phase, d - 1],
+            recv_sem=req_recv_sem.at[phase, d - 1],
+            device_id=(other, blk),
+            device_id_type=MESH,
+        )
 
     def req_exchange(phase, source_of, landing):
-        copies = []
-        for d in range(1, req_count):
-            other = lax.rem(req + d, req_count)
-            copy = pltpu.make_async_remote_copy(
-                src_ref=source_of(other),
-                dst_ref=landing.at[req],
-                send_sem=req_send_sem.at[phase, d - 1],
-                recv_sem=req_recv_sem.at[phase, d - 1],
-                device_id=(other, blk),
-                device_id_type=MESH,
-            )
+        copies = [
+            req_copy(phase, d, source_of(reqs[d]), landing, req, reqs[d])
+            for d in range(1, req_count)
+        ]
+        for copy in copies:
             copy.start()
-            copies.append(copy)
         return copies
 
     def req_arrivals(phase, source_of, landing):
         for d in range(1, req_count):
-            other = lax.rem(req + req_count - d, req_count)
+            other = reqs[req_count - d]
+            req_copy(phase, d, source_of(other), landing, other, other).wait_recv()
+
+    def all_exchange(phase, source_of, landing):
+        for peer in peers:
             pltpu.make_async_remote_copy(
-                src_ref=source_of(other),
-                dst_ref=landing.at[other],
-                send_sem=req_send_sem.at[phase, d - 1],
-                recv_sem=req_recv_sem.at[phase, d - 1],
-                device_id=(other, blk),
-                device_id_type=MESH,
-            ).wait_recv()
-
-    def all_exchange(phase, source_of, landing):
-        def send(i, carry):
-            other = lax.rem(me + i, everyone)
-            other_req = other // blk_count
-            pltpu.make_async_remote_copy(
-                src_ref=source_of(other, other_req),
+                src_ref=source_of(peer),
                 dst_ref=landing.at[me],
                 send_sem=all_send_sem.at[phase],
                 recv_sem=all_recv_sem.at[phase],
-                device_id=(other_req, lax.rem(other, blk_count)),
+                device_id=peer,
                 device_id_type=MESH,
             ).start()
-            return carry
-
-        lax.fori_loop(1, everyone, send, 0)
 
     def finish(copies):
         for copy in copies:
@@ -241,7 +229,8 @@
     ]
 
     blk_arrivals(0, lambda other: row_send, row_recv)
-    normed = gather_lanes(row_recv).astype(BF16)
+    wide_rows[...] = row_recv[...].astype(F32)
+    normed = gather_lanes(wide_rows).astype(BF16)
     projected = []
     for k in range(3):
         loads[k].wait()
@@ -281,12 +270,13 @@
         [mixed[h * group : (h + 1) * group] for h in range(heads)], axis=1
     )
     late[0].wait()
-    scatter_lanes(attn_send, jnp.dot(flat, wout[...], preferred_element_type=F32))
+    scatter_lanes(wide_rows, jnp.dot(flat, wout[...], preferred_element_type=F32))
+    attn_send[...] = wide_rows[...].astype(BF16)
 
     attn_copies = blk_exchange(1, lambda other: attn_send.at[other], attn_recv)
     attn_recv[blk] = attn_send[blk]
     blk_arrivals(1, lambda other: attn_send.at[other], attn_recv)
-    attn_out = functools.reduce(lambda a, b: a + b, [attn_recv[j] for j in range(blk_count)])
+    attn_out = functools.reduce(lambda a, b: a + b, [attn_recv[j].astype(F32) for j in range(blk_count)])
     state = [mixed_state[t] + depth_ref[0, t] * attn_out for t in range(count)]
     row = functools.reduce(lambda a, b: a + b, [state[s] * width_ref[1, s] for s in range(count)])
     row = normalize(row)
@@ -294,7 +284,7 @@
     for c in range(req_count):
         norm_send[c] = row[c * chunk : (c + 1) * chunk]
 
-    all_exchange(0, lambda other, other_req: norm_send.at[other_req], norm_recv)
+    all_exchange(0, lambda peer: norm_send.at[peer[0]], norm_recv)
     norm_recv[me] = norm_send[req]
     finish(attn_copies)
     mixed_state = [
@@ -306,29 +296,38 @@
     late[2].wait()
     wait_bytes(norm_recv.at[others], all_recv_sem.at[0])
     columns = gather_lanes(norm_recv).astype(BF16)
-    gate = jnp.dot(columns, wgate[...], preferred_element_type=F32)
-    up = jnp.dot(columns, wup[...], preferred_element_type=F32)
-    for c in range(req_count):
-        rows = slice(c * group, (c + 1) * group)
-        gate_send[c] = jnp.concatenate([gate[rows], up[rows]], axis=0).astype(BF16)
-
+    half = wgate.shape[1] // 2
+
+    def spread(part, landing):
+        for c in range(req_count):
+            rows = slice(c * group, (c + 1) * group)
+            landing[c] = jnp.concatenate([part[rows, :half], part[rows, half:]], axis=0).astype(
+                BF16
+            )
+
+    def total(landing):
+        return functools.reduce(
+            lambda a, b: a + b, [landing[c].astype(F32) for c in range(req_count)]
+        )
+
+    spread(jnp.dot(columns, wgate[...], preferred_element_type=F32), gate_send)
     gate_copies = req_exchange(0, lambda other: gate_send.at[other], gate_recv)
+    spread(jnp.dot(columns, wup[...], preferred_element_type=F32), up_send)
+    gate_copies += req_exchange(1, lambda other: up_send.at[other], up_recv)
     gate_recv[req] = gate_send[req]
+    up_recv[req] = up_send[req]
     wait_bytes(norm_recv.at[others], all_send_sem.at[0])
     req_arrivals(0, lambda other: gate_send.at[other], gate_recv)
-    both = functools.reduce(
-        lambda a, b: a + b, [gate_recv[c].astype(F32) for c in range(req_count)]
-    )
-    gate, up = both[:group], both[group:]
-    hidden = gate / (1.0 + jnp.exp(-gate)) * up
-    half = hidden.shape[1] // 2
-    hid_send[...] = jnp.concatenate([hidden[:, :half], hidden[:, half:]], axis=0).astype(BF16)
-
-    hid_copies = req_exchange(1, lambda other: hid_send, hid_recv)
+    gate = total(gate_recv)
+    gate = gate / (1.0 + jnp.exp(-gate))
+    req_arrivals(1, lambda other: up_send.at[other], up_recv)
+    hid_send[...] = (gate * total(up_recv)).astype(BF16)
+
+    hid_copies = req_exchange(2, lambda other: hid_send, hid_recv)
     hid_recv[req] = hid_send[...]
     finish(gate_copies)
     late[3].wait()
-    req_arrivals(1, lambda other: hid_send, hid_recv)
+    req_arrivals(2, lambda other: hid_send, hid_recv)
     stacked = hid_recv[...].reshape(req_count * 2 * group, half)
     first = jnp.dot(stacked, wdown[:half], preferred_element_type=F32)
     second = jnp.dot(stacked, wdown[half:], preferred_element_type=F32)
@@ -337,7 +336,7 @@
         part = first[low : low + group] + second[low + group : low + 2 * group]
         scatter_lanes(down_send.at[pl.ds(c * group, group)], part)
 
-    all_exchange(1, lambda other, other_req: down_send.at[other], down_recv)
+    all_exchange(1, lambda peer: down_send.at[peer[0] * blk_count + peer[1]], down_recv)
     down_recv[me] = down_send[me]
     finish(hid_copies)
     wait_bytes(down_recv.at[others], all_recv_sem.at[1])
@@ -347,9 +346,7 @@
         )
     mlp_out = mlp_row[...]
     for t in range(count):
-        streams[t] = mixed_state[t] + depth_ref[1, t] * mlp_out
-    for k in range(streams.shape[1]):
-        out_ref[0, :, k * LANES : (k + 1) * LANES] = streams[:, k, :]
+        out_ref[0, t] = mixed_state[t] + depth_ref[1, t] * mlp_out
     wait_bytes(down_recv.at[others], all_send_sem.at[1])
 
 
@@ -386,20 +383,23 @@
     big = [lines(key_cache), lines(value_cache), attn_in_weight, attn_out_weight, w_gate, w_up, w_down]
     return pl.pallas_call(
         functools.partial(layer_kernel, req_count, blk_count),
-        out_shape=jax.ShapeDtypeStruct(hyper_state.shape, hyper_state.dtype),
+        out_shape=jax.ShapeDtypeStruct((1, count, parts, LANES), F32),
         in_specs=[vmem, smem, vmem, smem, smem, smem] + [hbm] * len(big),
         out_specs=vmem,
         scratch_shapes=[like(x) for x in big]
         + [
             pltpu.VMEM((count, parts, LANES), F32),
-            pltpu.VMEM((parts, LANES), F32),
             pltpu.VMEM((blk_count, parts, LANES), F32),
-            pltpu.VMEM((blk_count, parts, LANES), F32),
-            pltpu.VMEM((blk_count, parts, LANES), F32),
+            pltpu.VMEM((parts, LANES), BF16),
+            pltpu.VMEM((blk_count, parts, LANES), BF16),
+            pltpu.VMEM((blk_count, parts, LANES), BF16),
+            pltpu.VMEM((blk_count, parts, LANES), BF16),
             pltpu.VMEM((req_count, chunk, LANES), F32),
             pltpu.VMEM((everyone, chunk, LANES), F32),
-            pltpu.VMEM((req_count, 2 * group, hid_part), BF16),
-            pltpu.VMEM((req_count, 2 * group, hid_part), BF16),
+            pltpu.VMEM((req_count, 2 * group, hid_part // 2), BF16),
+            pltpu.VMEM((req_count, 2 * group, hid_part // 2), BF16),
+            pltpu.VMEM((req_count, 2 * group, hid_part // 2), BF16),
+            pltpu.VMEM((req_count, 2 * group, hid_part // 2), BF16),
             pltpu.VMEM((2 * group, hid_part // 2), BF16),
             pltpu.VMEM((req_count, 2 * group, hid_part // 2), BF16),
             pltpu.VMEM((everyone, chunk, LANES), F32),
@@ -410,8 +410,8 @@
             dma((group,)),
             dma((2, blk_count - 1)),
             dma((2, blk_count - 1)),
-            dma((2, req_count - 1)),
-            dma((2, req_count - 1)),
+            dma((3, req_count - 1)),
+            dma((3, req_count - 1)),
             dma((2,)),
             dma((2,)),
         ],
@@ -419,7 +419,7 @@
             collective_id=0, has_side_effects=True, vmem_limit_bytes=56 * 2**20
         ),
         name="layer_step",
-    )(hyper_state, lengths, jnp.asarray(freqs), width_in, stream_mix, depth_out, *big)
+    )(hyper_state, lengths, jnp.asarray(freqs), width_in, stream_mix, depth_out, *big).reshape(hyper_state.shape)
 
 
 def solution(mesh):

time: 42.7 us -> 42.5 us (level)
    reshape x0 -> x1, local copies, waits for them, and re-layouts: none -> 1.39 us  [on_device(): return pl.pallas_call(functools.partial(layer_kernel, req_count, blk_coun...]
    unnamed x1 -> x0, local copies, waits for them, and re-layouts: 1.38 us -> none
where the time goes in v3:
time: 42.5 us; the launch traced here: 42.2 us
  Pallas kernels  40.8 us (96%)
  local copies, waits for them, and re-layouts  1.39 us (3%)
    pallas_call x1, Pallas kernels, on_device(): pl.pallas_call(functools.partial(layer_kernel, req_count, blk_count), out...  40.8 us
    reshape x1, local copies, waits for them, and re-layouts, on_device(): return pl.pallas_call(functools.partial(layer_kernel, req_count, blk_coun...  1.39 us

profile of v3, /device:TPU:0, one launch (start us, length us, event | category | flops | bytes accessed | tf_op | source)
XLA Modules:
  0.0 42.2 jit_solution(16128451383213379054)
XLA Ops:
  0.0 40.8 %layer_step.1 = f32[1,4,16,128]{3,2,1,0:T(8,128)} custom-call(f32[1,4,2048]{2,1,0:T(4,128)} %hyper_ref.1, s32[8]{0:T(128)} %lengths_ref.1, f32[1,128]{1,0:T(1,128)} %constant.2.clone.freq_ref, f32[2,4]{1,0:T(2,128)} %width_ref.1, f32[2,4,4]{2,1,0:T(4,128)} %mix_ref.1, f32[2,4]{1,0:T(2,128)} %depth_ref.1, bf16[8,4104,128]{2,1,0:T(8,128)(2,1)} %bitcast.8, ...), custom_call_target="tpu_custom_call" | custom-call | tf_op jit(solution)/shard_map/layer_step/pallas_call | solution.py:384
  40.8 1.4 %reshape.11 = f32[1,4,2048]{2,1,0:T(4,128)} reshape(f32[1,4,16,128]{3,2,1,0:T(8,128)} %layer_step.1) | data formatting | bytes 65536 | tf_op jit(solution)/shard_map/reshape | solution.py:422

commit v4 on v3

--- a/solution.py
+++ b/solution.py
@@ -52,12 +52,12 @@
 def layer_kernel(
     req_count,
     blk_count,
-    hyper_ref,
-    lengths_ref,
-    freq_ref,
-    width_ref,
-    mix_ref,
-    depth_ref,
+    hyper_hbm,
+    lengths_hbm,
+    freq_hbm,
+    width_hbm,
+    mix_hbm,
+    depth_hbm,
     keys_hbm,
     values_hbm,
     win_hbm,
@@ -66,6 +66,13 @@
     wup_hbm,
     wdown_hbm,
     out_ref,
+    hyper_ref,
+    lengths_ref,
+    freq_ref,
+    width_ref,
+    mix_ref,
+    depth_ref,
+    bias,
     keys,
     values,
     win,
@@ -90,6 +97,7 @@
     down_send,
     down_recv,
     mlp_row,
+    small_sem,
     load_sem,
     key_sem,
     value_sem,
@@ -107,6 +115,19 @@
     group, lines, head = keys.shape
     heads = win.shape[2] // head
 
+    small = [
+        pltpu.make_async_copy(src, dst, small_sem.at[i])
+        for i, (src, dst) in enumerate(
+            [
+                (hyper_hbm, hyper_ref),
+                (width_hbm, width_ref),
+                (lengths_hbm, lengths_ref),
+                (freq_hbm, freq_ref),
+                (mix_hbm, mix_ref),
+                (depth_hbm, depth_ref),
+            ]
+        )
+    ]
     loads = [pltpu.make_async_copy(win_hbm.at[k], win.at[k], load_sem.at[k]) for k in range(3)]
     key_loads = [
         pltpu.make_async_copy(keys_hbm.at[r], keys.at[r], key_sem.at[r]) for r in range(group)
@@ -128,12 +149,15 @@
     peers = [
         (reqs[i], blks[j]) for i in range(req_count) for j in range(blk_count) if i + j > 0
     ]
-    for copy in loads:
+    for copy in small + loads:
         copy.start()
     for peer in peers:
         pl.semaphore_signal(barrier, inc=1, device_id=peer, device_id_type=MESH)
     for copy in key_loads + value_loads + late:
         copy.start()
+
+    for copy in small:
+        copy.wait()
 
     for k in range(streams.shape[1]):
         streams[:, k, :] = hyper_ref[0, :, k * LANES : (k + 1) * LANES]
@@ -210,6 +234,14 @@
     row_copies = blk_exchange(0, lambda other: row_send, row_recv)
     row_recv[blk] = row_send[...]
 
+    def rotate(part):
+        return (part * cosine + pltpu.roll(part, head // 2, 1) * sine).astype(BF16)
+
+    mixed_state = [
+        functools.reduce(lambda a, b: a + b, [state[s] * mix_ref[0, s, t] for s in range(count)])
+        for t in range(count)
+    ]
+
     row_at = lax.broadcasted_iota(jnp.int32, (heads * group, 1), 0)
     request_at = lax.rem(row_at, group)
     lengths = jnp.zeros((heads * group, 1), jnp.int32)
@@ -220,13 +252,10 @@
     lane = lax.broadcasted_iota(jnp.int32, (heads * group, head), 1)
     sine = jnp.where(lane < head // 2, -sine, sine)
 
-    def rotate(part):
-        return (part * cosine + pltpu.roll(part, head // 2, 1) * sine).astype(BF16)
-
-    mixed_state = [
-        functools.reduce(lambda a, b: a + b, [state[s] * mix_ref[0, s, t] for s in range(count)])
-        for t in range(count)
-    ]
+    line = lax.broadcasted_iota(jnp.int32, (heads * group, lines), 1)
+    slot = line // heads
+    valid = (slot < lengths) & (line - slot * heads == row_at // group)
+    bias[...] = jnp.where(valid, 0.0, -jnp.inf)
 
     blk_arrivals(0, lambda other: row_send, row_recv)
     wide_rows[...] = row_recv[...].astype(F32)
@@ -245,27 +274,42 @@
     query = rotate(by_head(projected[0]))
     key_new = rotate(by_head(projected[1]))
     value_new = by_head(projected[2]).astype(BF16).astype(F32)
-    own = scale * jnp.sum(query.astype(F32) * key_new.astype(F32), axis=-1, keepdims=True)
-    for r in range(group):
+    wide_query = query.astype(F32)
+    own = scale * jnp.sum(wide_query * key_new.astype(F32), axis=-1, keepdims=True)
+    scores = None
+    for r in range(0, group, 2):
         key_loads[r].wait()
+        key_loads[r + 1].wait()
+        pair = jnp.concatenate(
+            [jnp.where(request_at == r + i, wide_query, 0.0) for i in range(2)], axis=1
+        ).astype(BF16)
         part = lax.dot_general(
-            query, keys[r], (((1,), (1,)), ((), ())), preferred_element_type=F32
-        )
-        scores = part if r == 0 else jnp.where(request_at == r, part, scores)
-    line = lax.broadcasted_iota(jnp.int32, (heads * group, lines), 1)
-    head_at = row_at // group
-    valid = (line < lengths * heads) & (lax.rem(line, heads) == head_at)
-    scores = jnp.where(valid, scores * scale, -jnp.inf)
+            pair,
+            jnp.concatenate([keys[r], keys[r + 1]], axis=1),
+            (((1,), (1,)), ((), ())),
+            preferred_element_type=F32,
+        )
+        scores = part if r == 0 else scores + part
+    scores = scores * scale + bias[...]
     peak = jnp.maximum(jnp.max(scores, axis=-1, keepdims=True), own)
     shares = jnp.exp(scores - peak)
     own_share = jnp.exp(own - peak)
     denom = jnp.sum(shares, axis=-1, keepdims=True) + own_share
     shares = shares.astype(BF16)
-    for r in range(group):
+    mixed = own_share * value_new
+    for r in range(0, group, 2):
         value_loads[r].wait()
-        part = jnp.dot(shares, values[r], preferred_element_type=F32)
-        mixed = part if r == 0 else jnp.where(request_at == r, part, mixed)
-    mixed = ((mixed + own_share * value_new) / denom).astype(BF16)
+        value_loads[r + 1].wait()
+        part = jnp.dot(
+            shares,
+            jnp.concatenate([values[r], values[r + 1]], axis=1),
+            preferred_element_type=F32,
+        )
+        for i in range(2):
+            mixed = mixed + jnp.where(
+                request_at == r + i, part[:, i * head : (i + 1) * head], 0.0
+            )
+    mixed = (mixed / denom).astype(BF16)
     flat = jnp.concatenate(
         [mixed[h * group : (h + 1) * group] for h in range(heads)], axis=1
     )
@@ -375,18 +419,27 @@
     freqs = np.exp(np.arange(head // 2) * (-2.0 * math.log(10000.0) / head))
     freqs = np.concatenate([freqs, freqs]).astype(np.float32)[None, :]
     vmem = pl.BlockSpec(memory_space=pltpu.VMEM)
-    smem = pl.BlockSpec(memory_space=pltpu.SMEM)
     hbm = pl.BlockSpec(memory_space=pl.ANY)
     like = lambda x: pltpu.VMEM(x.shape, x.dtype)
+    scalars = lambda x: pltpu.SMEM(x.shape, x.dtype)
     dma = pltpu.SemaphoreType.DMA
     lines = lambda x: jnp.transpose(x, (0, 2, 1, 3)).reshape(group, slots * heads, head)
     big = [lines(key_cache), lines(value_cache), attn_in_weight, attn_out_weight, w_gate, w_up, w_down]
     return pl.pallas_call(
         functools.partial(layer_kernel, req_count, blk_count),
         out_shape=jax.ShapeDtypeStruct((1, count, parts, LANES), F32),
-        in_specs=[vmem, smem, vmem, smem, smem, smem] + [hbm] * len(big),
+        in_specs=[hbm] * (6 + len(big)),
         out_specs=vmem,
-        scratch_shapes=[like(x) for x in big]
+        scratch_shapes=[
+            like(hyper_state),
+            scalars(lengths),
+            pltpu.VMEM(freqs.shape, F32),
+            scalars(width_in),
+            scalars(stream_mix),
+            scalars(depth_out),
+            pltpu.VMEM((heads * group, slots * heads), F32),
+        ]
+        + [like(x) for x in big]
         + [
             pltpu.VMEM((count, parts, LANES), F32),
             pltpu.VMEM((blk_count, parts, LANES), F32),
@@ -405,6 +458,7 @@
             pltpu.VMEM((everyone, chunk, LANES), F32),
             pltpu.VMEM((everyone, chunk, LANES), F32),
             pltpu.VMEM((parts, LANES), F32),
+            dma((6,)),
             dma((7,)),
             dma((group,)),
             dma((group,)),

time: 42.5 us -> 42 us (0.988)
  no operation moved by 1% of the time
where the time goes in v4:
time: 42 us; the launch traced here: 41.9 us
  Pallas kernels  40.5 us (96%)
  local copies, waits for them, and re-layouts  1.39 us (3%)
    pallas_call x1, Pallas kernels, on_device(): pl.pallas_call(functools.partial(layer_kernel, req_count, blk_count), out...  40.5 us
    reshape x1, local copies, waits for them, and re-layouts, on_device(): return pl.pallas_call(functools.partial(layer_kernel, req_count, blk_coun...  1.39 us

profile of v4, /device:TPU:0, one launch (start us, length us, event | category | flops | bytes accessed | tf_op | source)
XLA Modules:
  0.0 41.9 jit_solution(11753164437260026735)
XLA Ops:
  0.0 40.5 %layer_step.1 = f32[1,4,16,128]{3,2,1,0:T(8,128)} custom-call(f32[1,4,2048]{2,1,0:T(4,128)} %hyper_hbm.1, s32[8]{0:T(128)} %lengths_hbm.1, f32[1,128]{1,0:T(1,128)} %constant.2.clone.freq_hbm, f32[2,4]{1,0:T(2,128)} %width_hbm.1, f32[2,4,4]{2,1,0:T(4,128)} %mix_hbm.1, f32[2,4]{1,0:T(2,128)} %depth_hbm.1, bf16[8,4104,128]{2,1,0:T(8,128)(2,1)} %bitcast.8, ...), custom_call_target="tpu_custom_call" | custom-call | tf_op jit(solution)/shard_map/layer_step/pallas_call | solution.py:428
  40.5 1.4 %reshape.11 = f32[1,4,2048]{2,1,0:T(4,128)} reshape(f32[1,4,16,128]{3,2,1,0:T(8,128)} %layer_step.1) | data formatting | bytes 65536 | tf_op jit(solution)/shard_map/reshape | solution.py:476

commit v5 on v4

--- a/solution.py
+++ b/solution.py
@@ -43,10 +43,6 @@
 def scatter_lanes(ref, values):
     for k in range(ref.shape[1]):
         ref[:, k, :] = values[:, k * LANES : (k + 1) * LANES]
-
-
-def wait_bytes(ref, sem):
-    pltpu.make_async_copy(ref, ref, sem).wait()
 
 
 def layer_kernel(
@@ -96,7 +92,11 @@
     hid_recv,
     down_send,
     down_recv,
-    mlp_row,
+    part_send,
+    part_recv,
+    last_send,
+    last_recv,
+    joined,
     small_sem,
     load_sem,
     key_sem,
@@ -105,13 +105,9 @@
     blk_recv_sem,
     req_send_sem,
     req_recv_sem,
-    all_send_sem,
-    all_recv_sem,
 ):
     req = lax.axis_index("req")
     blk = lax.axis_index("blk")
-    everyone = req_count * blk_count
-    me = req * blk_count + blk
     group, lines, head = keys.shape
     heads = win.shape[2] // head
 
@@ -146,9 +142,7 @@
 
     reqs = [req] + [lax.rem(req + d, req_count) for d in range(1, req_count)]
     blks = [blk] + [lax.rem(blk + d, blk_count) for d in range(1, blk_count)]
-    peers = [
-        (reqs[i], blks[j]) for i in range(req_count) for j in range(blk_count) if i + j > 0
-    ]
+    peers = [(req, other) for other in blks[1:]] + [(other, blk) for other in reqs[1:]]
     for copy in small + loads:
         copy.start()
     for peer in peers:
@@ -166,7 +160,7 @@
     row = functools.reduce(lambda a, b: a + b, [state[s] * width_ref[0, s] for s in range(count)])
     row_send[...] = normalize(row).astype(BF16)
 
-    pl.semaphore_wait(barrier, everyone - 1)
+    pl.semaphore_wait(barrier, len(peers))
 
     def blk_copy(phase, d, source, landing, slot, other):
         return pltpu.make_async_remote_copy(
@@ -215,17 +209,6 @@
         for d in range(1, req_count):
             other = reqs[req_count - d]
             req_copy(phase, d, source_of(other), landing, other, other).wait_recv()
-
-    def all_exchange(phase, source_of, landing):
-        for peer in peers:
-            pltpu.make_async_remote_copy(
-                src_ref=source_of(peer),
-                dst_ref=landing.at[me],
-                send_sem=all_send_sem.at[phase],
-                recv_sem=all_recv_sem.at[phase],
-                device_id=peer,
-                device_id_type=MESH,
-            ).start()
 
     def finish(copies):
         for copy in copies:
@@ -328,18 +311,31 @@
     for c in range(req_count):
         norm_send[c] = row[c * chunk : (c + 1) * chunk]
 
-    all_exchange(0, lambda peer: norm_send.at[peer[0]], norm_recv)
-    norm_recv[me] = norm_send[req]
+    norm_copies = req_exchange(3, lambda other: norm_send.at[other], norm_recv)
+    norm_recv[req] = norm_send[req]
     finish(attn_copies)
+    req_arrivals(3, lambda other: norm_send.at[other], norm_recv)
+    for c in range(req_count):
+        joined[c * chunk : (c + 1) * chunk] = norm_recv[c]
+    part_send[...] = joined[...].astype(BF16)
+    part_copies = blk_exchange(2, lambda other: part_send, part_recv)
+    part_recv[blk] = part_send[...]
+    finish(norm_copies)
     mixed_state = [
         functools.reduce(lambda a, b: a + b, [state[s] * mix_ref[1, s, t] for s in range(count)])
         for t in range(count)
     ]
-    others = pl.ds(0, everyone - 1)
     late[1].wait()
     late[2].wait()
-    wait_bytes(norm_recv.at[others], all_recv_sem.at[0])
-    columns = gather_lanes(norm_recv).astype(BF16)
+    blk_arrivals(2, lambda other: part_send, part_recv)
+    wide_rows[...] = part_recv[...].astype(F32)
+    columns = jnp.concatenate(
+        [
+            jnp.concatenate([wide_rows[:, c * chunk + k, :] for k in range(chunk)], axis=1)
+            for c in range(req_count)
+        ],
+        axis=0,
+    ).astype(BF16)
     half = wgate.shape[1] // 2
 
     def spread(part, landing):
@@ -360,7 +356,7 @@
     gate_copies += req_exchange(1, lambda other: up_send.at[other], up_recv)
     gate_recv[req] = gate_send[req]
     up_recv[req] = up_send[req]
-    wait_bytes(norm_recv.at[others], all_send_sem.at[0])
+    finish(part_copies)
     req_arrivals(0, lambda other: gate_send.at[other], gate_recv)
     gate = total(gate_recv)
     gate = gate / (1.0 + jnp.exp(-gate))
@@ -378,20 +374,29 @@
     for c in range(req_count):
         low = 2 * group * c
         part = first[low : low + group] + second[low + group : low + 2 * group]
-        scatter_lanes(down_send.at[pl.ds(c * group, group)], part)
-
-    all_exchange(1, lambda peer: down_send.at[peer[0] * blk_count + peer[1]], down_recv)
-    down_recv[me] = down_send[me]
+        for k in range(chunk):
+            wide_rows[:, c * chunk + k, :] = part[:, k * LANES : (k + 1) * LANES]
+    down_send[...] = wide_rows[...].astype(BF16)
+
+    down_copies = blk_exchange(3, lambda other: down_send.at[other], down_recv)
+    down_recv[blk] = down_send[blk]
     finish(hid_copies)
-    wait_bytes(down_recv.at[others], all_recv_sem.at[1])
+    blk_arrivals(3, lambda other: down_send.at[other], down_recv)
+    joined[...] = functools.reduce(
+        lambda a, b: a + b, [down_recv[j].astype(F32) for j in range(blk_count)]
+    )
     for c in range(req_count):
-        mlp_row[c * chunk : (c + 1) * chunk] = functools.reduce(
-            lambda a, b: a + b, [down_recv[c * blk_count + j] for j in range(blk_count)]
-        )
-    mlp_out = mlp_row[...]
+        last_send[c] = joined[c * chunk : (c + 1) * chunk]
+    last_copies = req_exchange(4, lambda other: last_send.at[other], last_recv)
+    last_recv[req] = last_send[req]
+    finish(down_copies)
+    req_arrivals(4, lambda other: last_send.at[other], last_recv)
+    for c in range(req_count):
+        joined[c * chunk : (c + 1) * chunk] = last_recv[c]
+    mlp_out = joined[...]
     for t in range(count):
         out_ref[0, t] = mixed_state[t] + depth_ref[1, t] * mlp_out
-    wait_bytes(down_recv.at[others], all_send_sem.at[1])
+    finish(last_copies)
 
 
 def on_device(
@@ -410,7 +415,6 @@
 ):
     req_count = lax.axis_size("req")
     blk_count = lax.axis_size("blk")
-    everyone = req_count * blk_count
     _, count, width = hyper_state.shape
     group, heads, slots, head = key_cache.shape
     feature_part, hid_part = w_gate.shape
@@ -448,26 +452,28 @@
             pltpu.VMEM((blk_count, parts, LANES), BF16),
             pltpu.VMEM((blk_count, parts, LANES), BF16),
             pltpu.VMEM((req_count, chunk, LANES), F32),
-            pltpu.VMEM((everyone, chunk, LANES), F32),
+            pltpu.VMEM((req_count, chunk, LANES), F32),
             pltpu.VMEM((req_count, 2 * group, hid_part // 2), BF16),
             pltpu.VMEM((req_count, 2 * group, hid_part // 2), BF16),
             pltpu.VMEM((req_count, 2 * group, hid_part // 2), BF16),
             pltpu.VMEM((req_count, 2 * group, hid_part // 2), BF16),
             pltpu.VMEM((2 * group, hid_part // 2), BF16),
             pltpu.VMEM((req_count, 2 * group, hid_part // 2), BF16),
-            pltpu.VMEM((everyone, chunk, LANES), F32),
-            pltpu.VMEM((everyone, chunk, LANES), F32),
+            pltpu.VMEM((blk_count, parts, LANES), BF16),
+            pltpu.VMEM((blk_count, parts, LANES), BF16),
+            pltpu.VMEM((parts, LANES), BF16),
+            pltpu.VMEM((blk_count, parts, LANES), BF16),
+            pltpu.VMEM((req_count, chunk, LANES), F32),
+            pltpu.VMEM((req_count, chunk, LANES), F32),
             pltpu.VMEM((parts, LANES), F32),
             dma((6,)),
             dma((7,)),
             dma((group,)),
             dma((group,)),
-            dma((2, blk_count - 1)),
-            dma((2, blk_count - 1)),
-            dma((3, req_count - 1)),
-            dma((3, req_count - 1)),
-            dma((2,)),
-            dma((2,)),
+            dma((4, blk_count - 1)),
+            dma((4, blk_count - 1)),
+            dma((5, req_count - 1)),
+            dma((5, req_count - 1)),
         ],
         compiler_params=pltpu.CompilerParams(
             collective_id=0, has_side_effects=True, vmem_limit_bytes=56 * 2**20

time: 42 us -> 44.6 us (1.062)
  Pallas kernels: 40.5 us -> 43 us
    pallas_call x1, Pallas kernels: 40.5 us -> 43 us  [on_device(): pl.pallas_call(functools.partial(layer_kernel, req_count, blk_count), out...]
where the time goes in v5:
time: 44.6 us; the launch traced here: 44.4 us
  Pallas kernels  43 us (96%)
  local copies, waits for them, and re-layouts  1.39 us (3%)
    pallas_call x1, Pallas kernels, on_device(): pl.pallas_call(functools.partial(layer_kernel, req_count, blk_count), out...  43 us
    reshape x1, local copies, waits for them, and re-layouts, on_device(): return pl.pallas_call(functools.partial(layer_kernel, req_count, blk_coun...  1.39 us

profile of v5, /device:TPU:0, one launch (start us, length us, event | category | flops | bytes accessed | tf_op | source)
XLA Modules:
  0.0 44.4 jit_solution(17072020981316641094)
XLA Ops:
  0.0 43.0 %layer_step.1 = f32[1,4,16,128]{3,2,1,0:T(8,128)} custom-call(f32[1,4,2048]{2,1,0:T(4,128)} %hyper_hbm.1, s32[8]{0:T(128)} %lengths_hbm.1, f32[1,128]{1,0:T(1,128)} %constant.2.clone.freq_hbm, f32[2,4]{1,0:T(2,128)} %width_hbm.1, f32[2,4,4]{2,1,0:T(4,128)} %mix_hbm.1, f32[2,4]{1,0:T(2,128)} %depth_hbm.1, bf16[8,4104,128]{2,1,0:T(8,128)(2,1)} %bitcast.8, ...), custom_call_target="tpu_custom_call" | custom-call | tf_op jit(solution)/shard_map/layer_step/pallas_call | solution.py:432
  43.0 1.4 %reshape.11 = f32[1,4,2048]{2,1,0:T(4,128)} reshape(f32[1,4,16,128]{3,2,1,0:T(8,128)} %layer_step.1) | data formatting | bytes 65536 | tf_op jit(solution)/shard_map/reshape | solution.py:482

commit v6 on v4

--- a/solution.py
+++ b/solution.py
@@ -92,11 +92,9 @@
     gate_recv,
     up_send,
     up_recv,
-    hid_send,
-    hid_recv,
+    wide_down,
     down_send,
     down_recv,
-    mlp_row,
     small_sem,
     load_sem,
     key_sem,
@@ -136,10 +134,15 @@
         pltpu.make_async_copy(values_hbm.at[r], values.at[r], value_sem.at[r])
         for r in range(group)
     ]
+    sub = wdown.shape[1]
+
+    def down_block(other):
+        return wdown_hbm.at[pl.ds(pl.multiple_of(other * sub, sub), sub)]
+
     late = [
         pltpu.make_async_copy(src, dst, load_sem.at[3 + i])
         for i, (src, dst) in enumerate(
-            [(wout_hbm, wout), (wgate_hbm, wgate), (wup_hbm, wup), (wdown_hbm, wdown)]
+            [(wout_hbm, wout), (wgate_hbm, wgate), (wup_hbm, wup), (down_block(req), wdown.at[req])]
         )
     ]
     barrier = pltpu.get_barrier_semaphore()
@@ -153,7 +156,7 @@
         copy.start()
     for peer in peers:
         pl.semaphore_signal(barrier, inc=1, device_id=peer, device_id_type=MESH)
-    for copy in key_loads + value_loads + late:
+    for copy in key_loads:
         copy.start()
 
     for copy in small:
@@ -232,6 +235,9 @@
             copy.wait_send()
 
     row_copies = blk_exchange(0, lambda other: row_send, row_recv)
+    for copy in value_loads + late:
+        copy.start()
+    weight_copies = req_exchange(2, down_block, wdown)
     row_recv[blk] = row_send[...]
 
     def rotate(part):
@@ -340,14 +346,10 @@
     late[2].wait()
     wait_bytes(norm_recv.at[others], all_recv_sem.at[0])
     columns = gather_lanes(norm_recv).astype(BF16)
-    half = wgate.shape[1] // 2
 
     def spread(part, landing):
         for c in range(req_count):
-            rows = slice(c * group, (c + 1) * group)
-            landing[c] = jnp.concatenate([part[rows, :half], part[rows, half:]], axis=0).astype(
-                BF16
-            )
+            landing[c] = part[:, c * sub : (c + 1) * sub].astype(BF16)
 
     def total(landing):
         return functools.reduce(
@@ -365,30 +367,23 @@
     gate = total(gate_recv)
     gate = gate / (1.0 + jnp.exp(-gate))
     req_arrivals(1, lambda other: up_send.at[other], up_recv)
-    hid_send[...] = (gate * total(up_recv)).astype(BF16)
-
-    hid_copies = req_exchange(2, lambda other: hid_send, hid_recv)
-    hid_recv[req] = hid_send[...]
-    finish(gate_copies)
+    hidden = (gate * total(up_recv)).astype(BF16)
+
+    finish(weight_copies)
     late[3].wait()
-    req_arrivals(2, lambda other: hid_send, hid_recv)
-    stacked = hid_recv[...].reshape(req_count * 2 * group, half)
-    first = jnp.dot(stacked, wdown[:half], preferred_element_type=F32)
-    second = jnp.dot(stacked, wdown[half:], preferred_element_type=F32)
+    req_arrivals(2, down_block, wdown)
     for c in range(req_count):
-        low = 2 * group * c
-        part = first[low : low + group] + second[low + group : low + 2 * group]
-        scatter_lanes(down_send.at[pl.ds(c * group, group)], part)
-
+        part = jnp.dot(hidden, wdown[c], preferred_element_type=F32)
+        for k in range(chunk):
+            wide_down[:, c * chunk + k, :] = part[:, k * LANES : (k + 1) * LANES]
+    down_send[...] = wide_down[...].astype(BF16)
     all_exchange(1, lambda peer: down_send.at[peer[0] * blk_count + peer[1]], down_recv)
     down_recv[me] = down_send[me]
-    finish(hid_copies)
+    finish(gate_copies)
     wait_bytes(down_recv.at[others], all_recv_sem.at[1])
-    for c in range(req_count):
-        mlp_row[c * chunk : (c + 1) * chunk] = functools.reduce(
-            lambda a, b: a + b, [down_recv[c * blk_count + j] for j in range(blk_count)]
-        )
-    mlp_out = mlp_row[...]
+    mlp_out = functools.reduce(
+        lambda a, b: a + b, [down_recv[j].astype(F32) for j in range(everyone)]
+    )
     for t in range(count):
         out_ref[0, t] = mixed_state[t] + depth_ref[1, t] * mlp_out
     wait_bytes(down_recv.at[others], all_send_sem.at[1])
@@ -415,6 +410,7 @@
     group, heads, slots, head = key_cache.shape
     feature_part, hid_part = w_gate.shape
     parts = width // LANES
+    sub = hid_part // req_count
     chunk = feature_part // LANES
     freqs = np.exp(np.arange(head // 2) * (-2.0 * math.log(10000.0) / head))
     freqs = np.concatenate([freqs, freqs]).astype(np.float32)[None, :]
@@ -439,7 +435,8 @@
             scalars(depth_out),
             pltpu.VMEM((heads * group, slots * heads), F32),
         ]
-        + [like(x) for x in big]
+        + [like(x) for x in big[:-1]]
+        + [pltpu.VMEM((req_count, sub, w_down.shape[1]), BF16)]
         + [
             pltpu.VMEM((count, parts, LANES), F32),
             pltpu.VMEM((blk_count, parts, LANES), F32),
@@ -449,15 +446,13 @@
             pltpu.VMEM((blk_count, parts, LANES), BF16),
             pltpu.VMEM((req_count, chunk, LANES), F32),
             pltpu.VMEM((everyone, chunk, LANES), F32),
-            pltpu.VMEM((req_count, 2 * group, hid_part // 2), BF16),
-            pltpu.VMEM((req_count, 2 * group, hid_part // 2), BF16),
-            pltpu.VMEM((req_count, 2 * group, hid_part // 2), BF16),
-            pltpu.VMEM((req_count, 2 * group, hid_part // 2), BF16),
-            pltpu.VMEM((2 * group, hid_part // 2), BF16),
-            pltpu.VMEM((req_count, 2 * group, hid_part // 2), BF16),
-            pltpu.VMEM((everyone, chunk, LANES), F32),
-            pltpu.VMEM((everyone, chunk, LANES), F32),
-            pltpu.VMEM((parts, LANES), F32),
+            pltpu.VMEM((req_count, everyone, sub), BF16),
+            pltpu.VMEM((req_count, everyone, sub), BF16),
+            pltpu.VMEM((req_count, everyone, sub), BF16),
+            pltpu.VMEM((req_count, everyone, sub), BF16),
+            pltpu.VMEM((everyone, parts, LANES), F32),
+            pltpu.VMEM((everyone, parts, LANES), BF16),
+            pltpu.VMEM((everyone, parts, LANES), BF16),
             dma((6,)),
             dma((7,)),
             dma((group,)),

time: 42 us -> 38.7 us (0.921)
  Pallas kernels: 40.5 us -> 37.1 us
    pallas_call x1, Pallas kernels: 40.5 us -> 37.1 us  [on_device(): pl.pallas_call(functools.partial(layer_kernel, req_count, blk_count), out...]
where the time goes in v6:
time: 38.7 us; the launch traced here: 38.5 us
  Pallas kernels  37.1 us (96%)
  local copies, waits for them, and re-layouts  1.39 us (4%)
    pallas_call x1, Pallas kernels, on_device(): pl.pallas_call(functools.partial(layer_kernel, req_count, blk_count), out...  37.1 us
    reshape x1, local copies, waits for them, and re-layouts, on_device(): return pl.pallas_call(functools.partial(layer_kernel, req_count, blk_coun...  1.39 us

profile of v6, /device:TPU:0, one launch (start us, length us, event | category | flops | bytes accessed | tf_op | source)
XLA Modules:
  0.0 38.5 jit_solution(16317794359045316283)
XLA Ops:
  0.0 37.1 %layer_step.1 = f32[1,4,16,128]{3,2,1,0:T(8,128)} custom-call(f32[1,4,2048]{2,1,0:T(4,128)} %hyper_hbm.1, s32[8]{0:T(128)} %lengths_hbm.1, f32[1,128]{1,0:T(1,128)} %constant.2.clone.freq_hbm, f32[2,4]{1,0:T(2,128)} %width_hbm.1, f32[2,4,4]{2,1,0:T(4,128)} %mix_hbm.1, f32[2,4]{1,0:T(2,128)} %depth_hbm.1, bf16[8,4104,128]{2,1,0:T(8,128)(2,1)} %bitcast.8, ...), custom_call_target="tpu_custom_call" | custom-call | tf_op jit(solution)/shard_map/layer_step/pallas_call | solution.py:424
  37.1 1.4 %reshape.11 = f32[1,4,2048]{2,1,0:T(4,128)} reshape(f32[1,4,16,128]{3,2,1,0:T(8,128)} %layer_step.1) | data formatting | bytes 65536 | tf_op jit(solution)/shard_map/reshape | solution.py:471

commit v7 on v6

--- a/solution.py
+++ b/solution.py
@@ -73,6 +73,7 @@
     mix_ref,
     depth_ref,
     bias,
+    keys_turned,
     keys,
     values,
     win,
@@ -263,6 +264,10 @@
     valid = (slot < lengths) & (line - slot * heads == row_at // group)
     bias[...] = jnp.where(valid, 0.0, -jnp.inf)
 
+    for r in range(group):
+        key_loads[r].wait()
+        keys_turned[r] = jnp.transpose(keys[r])
+
     blk_arrivals(0, lambda other: row_send, row_recv)
     wide_rows[...] = row_recv[...].astype(F32)
     normed = gather_lanes(wide_rows).astype(BF16)
@@ -284,15 +289,12 @@
     own = scale * jnp.sum(wide_query * key_new.astype(F32), axis=-1, keepdims=True)
     scores = None
     for r in range(0, group, 2):
-        key_loads[r].wait()
-        key_loads[r + 1].wait()
         pair = jnp.concatenate(
             [jnp.where(request_at == r + i, wide_query, 0.0) for i in range(2)], axis=1
         ).astype(BF16)
-        part = lax.dot_general(
+        part = jnp.dot(
             pair,
-            jnp.concatenate([keys[r], keys[r + 1]], axis=1),
-            (((1,), (1,)), ((), ())),
+            jnp.concatenate([keys_turned[r], keys_turned[r + 1]], axis=0),
             preferred_element_type=F32,
         )
         scores = part if r == 0 else scores + part
@@ -434,6 +436,7 @@
             scalars(stream_mix),
             scalars(depth_out),
             pltpu.VMEM((heads * group, slots * heads), F32),
+            pltpu.VMEM((group, head, slots * heads), BF16),
         ]
         + [like(x) for x in big[:-1]]
         + [pltpu.VMEM((req_count, sub, w_down.shape[1]), BF16)]

time: 38.7 us -> 37.3 us (0.964)
  Pallas kernels: 37.1 us -> 35.7 us
    pallas_call x1, Pallas kernels: 37.1 us -> 35.7 us  [on_device(): pl.pallas_call(functools.partial(layer_kernel, req_count, blk_count), out...]
where the time goes in v7:
time: 37.3 us; the launch traced here: 37.1 us
  Pallas kernels  35.7 us (96%)
  local copies, waits for them, and re-layouts  1.39 us (4%)
    pallas_call x1, Pallas kernels, on_device(): pl.pallas_call(functools.partial(layer_kernel, req_count, blk_count), out...  35.7 us
    reshape x1, local copies, waits for them, and re-layouts, on_device(): return pl.pallas_call(functools.partial(layer_kernel, req_count, blk_coun...  1.39 us

profile of v7, /device:TPU:0, one launch (start us, length us, event | category | flops | bytes accessed | tf_op | source)
XLA Modules:
  0.0 37.1 jit_solution(6038066540747388876)
XLA Ops:
  0.0 35.7 %layer_step.1 = f32[1,4,16,128]{3,2,1,0:T(8,128)} custom-call(f32[1,4,2048]{2,1,0:T(4,128)} %hyper_hbm.1, s32[8]{0:T(128)} %lengths_hbm.1, f32[1,128]{1,0:T(1,128)} %constant.2.clone.freq_hbm, f32[2,4]{1,0:T(2,128)} %width_hbm.1, f32[2,4,4]{2,1,0:T(4,128)} %mix_hbm.1, f32[2,4]{1,0:T(2,128)} %depth_hbm.1, bf16[8,4104,128]{2,1,0:T(8,128)(2,1)} %bitcast.8, ...), custom_call_target="tpu_custom_call" | custom-call | tf_op jit(solution)/shard_map/layer_step/pallas_call | solution.py:426
  35.7 1.4 %reshape.11 = f32[1,4,2048]{2,1,0:T(4,128)} reshape(f32[1,4,16,128]{3,2,1,0:T(8,128)} %layer_step.1) | data formatting | bytes 65536 | tf_op jit(solution)/shard_map/reshape | solution.py:474

commit v8 on v7

--- a/solution.py
+++ b/solution.py
@@ -132,7 +132,9 @@
         pltpu.make_async_copy(keys_hbm.at[r], keys.at[r], key_sem.at[r]) for r in range(group)
     ]
     value_loads = [
-        pltpu.make_async_copy(values_hbm.at[r], values.at[r], value_sem.at[r])
+        pltpu.make_async_copy(
+            values_hbm.at[r], values.at[:, pl.ds(r * head, head)], value_sem.at[r]
+        )
         for r in range(group)
     ]
     sub = wdown.shape[1]
@@ -266,7 +268,7 @@
 
     for r in range(group):
         key_loads[r].wait()
-        keys_turned[r] = jnp.transpose(keys[r])
+        keys_turned[r * head : (r + 1) * head] = jnp.transpose(keys[r])
 
     blk_arrivals(0, lambda other: row_send, row_recv)
     wide_rows[...] = row_recv[...].astype(F32)
@@ -287,17 +289,10 @@
     value_new = by_head(projected[2]).astype(BF16).astype(F32)
     wide_query = query.astype(F32)
     own = scale * jnp.sum(wide_query * key_new.astype(F32), axis=-1, keepdims=True)
-    scores = None
-    for r in range(0, group, 2):
-        pair = jnp.concatenate(
-            [jnp.where(request_at == r + i, wide_query, 0.0) for i in range(2)], axis=1
-        ).astype(BF16)
-        part = jnp.dot(
-            pair,
-            jnp.concatenate([keys_turned[r], keys_turned[r + 1]], axis=0),
-            preferred_element_type=F32,
-        )
-        scores = part if r == 0 else scores + part
+    spread_query = jnp.concatenate(
+        [jnp.where(request_at == r, wide_query, 0.0) for r in range(group)], axis=1
+    ).astype(BF16)
+    scores = jnp.dot(spread_query, keys_turned[...], preferred_element_type=F32)
     scores = scores * scale + bias[...]
     peak = jnp.maximum(jnp.max(scores, axis=-1, keepdims=True), own)
     shares = jnp.exp(scores - peak)
@@ -305,18 +300,13 @@
     denom = jnp.sum(shares, axis=-1, keepdims=True) + own_share
     shares = shares.astype(BF16)
     mixed = own_share * value_new
-    for r in range(0, group, 2):
+    for r in range(group):
         value_loads[r].wait()
-        value_loads[r + 1].wait()
-        part = jnp.dot(
-            shares,
-            jnp.concatenate([values[r], values[r + 1]], axis=1),
-            preferred_element_type=F32,
-        )
-        for i in range(2):
-            mixed = mixed + jnp.where(
-                request_at == r + i, part[:, i * head : (i + 1) * head], 0.0
-            )
+    part = jnp.dot(shares, values[...], preferred_element_type=F32)
+    for r in range(group):
+        mixed = mixed + jnp.where(
+            request_at == r, part[:, r * head : (r + 1) * head], 0.0
+        )
     mixed = (mixed / denom).astype(BF16)
     flat = jnp.concatenate(
         [mixed[h * group : (h + 1) * group] for h in range(heads)], axis=1
@@ -436,9 +426,10 @@
             scalars(stream_mix),
             scalars(depth_out),
             pltpu.VMEM((heads * group, slots * heads), F32),
-            pltpu.VMEM((group, head, slots * heads), BF16),
+            pltpu.VMEM((group * head, slots * heads), BF16),
         ]
-        + [like(x) for x in big[:-1]]
+        + [like(big[0]), pltpu.VMEM((slots * heads, group * head), BF16)]
+        + [like(x) for x in big[2:-1]]
         + [pltpu.VMEM((req_count, sub, w_down.shape[1]), BF16)]
         + [
             pltpu.VMEM((count, parts, LANES), F32),

time: 37.3 us -> 35.3 us (0.946)
  Pallas kernels: 35.7 us -> 33.8 us
    pallas_call x1, Pallas kernels: 35.7 us -> 33.8 us  [on_device(): pl.pallas_call(functools.partial(layer_kernel, req_count, blk_count), out...]
where the time goes in v8:
time: 35.3 us; the launch traced here: 35.2 us
  Pallas kernels  33.8 us (96%)
  local copies, waits for them, and re-layouts  1.39 us (4%)
    pallas_call x1, Pallas kernels, on_device(): pl.pallas_call(functools.partial(layer_kernel, req_count, blk_count), out...  33.8 us
    reshape x1, local copies, waits for them, and re-layouts, on_device(): return pl.pallas_call(functools.partial(layer_kernel, req_count, blk_coun...  1.39 us

profile of v8, /device:TPU:0, one launch (start us, length us, event | category | flops | bytes accessed | tf_op | source)
XLA Modules:
  0.0 35.2 jit_solution(5338267517831404872)
XLA Ops:
  0.0 33.8 %layer_step.1 = f32[1,4,16,128]{3,2,1,0:T(8,128)} custom-call(f32[1,4,2048]{2,1,0:T(4,128)} %hyper_hbm.1, s32[8]{0:T(128)} %lengths_hbm.1, f32[1,128]{1,0:T(1,128)} %constant.2.clone.freq_hbm, f32[2,4]{1,0:T(2,128)} %width_hbm.1, f32[2,4,4]{2,1,0:T(4,128)} %mix_hbm.1, f32[2,4]{1,0:T(2,128)} %depth_hbm.1, bf16[8,4104,128]{2,1,0:T(8,128)(2,1)} %bitcast.8, ...), custom_call_target="tpu_custom_call" | custom-call | tf_op jit(solution)/shard_map/layer_step/pallas_call | solution.py:416
  33.8 1.4 %reshape.11 = f32[1,4,2048]{2,1,0:T(4,128)} reshape(f32[1,4,16,128]{3,2,1,0:T(8,128)} %layer_step.1) | data formatting | bytes 65536 | tf_op jit(solution)/shard_map/reshape | solution.py:465
